TPU v7x, 128 devices: a whole 4x4x4 slice. The times are simulated.
128 devices in a mesh: slab: 32 (over y, z_hi, x), comp: 4 (over z_lo, core).
Axes of the slice: x: 4, y: 4, z: 4 (z_hi: 2, z_lo: 2; z = z_hi * 2 + z_lo), core: 2. Of those that a mesh axis runs over, the one named last changes fastest.
Arguments:
- current_field: float32 [3, 256, 64, 256], P(None, 'slab', 'comp'), may hold values from -6 to 6
- earlier_field: float32 [3, 256, 64, 256], P(None, 'slab', 'comp'), may hold values from -6 to 6
- wave_coef: float32 [256, 64, 256], P('slab', 'comp'), may hold values from 0.05 to 0.24
- layer_mask: int32 [256, 64, 256], P('slab', 'comp'), may hold values from 0 to 2
- point_xyz: float32 [3, 131072], P(None, ('slab', 'comp')), may hold values from 0 to 4
- point_owner: int32 [131072, 1], P(('slab', 'comp')), may hold values from 0 to 127; in each aligned block of 1024 rows (0 to 1023, 1024 to 2047, ...) at most 16 rows name the same one
- cell_offset: int32 [131072], P(('slab', 'comp')), may hold values from 0 to 32767
- wave_vector: float32 [3, 4096], P(None, 'comp'), may hold values from -8 to 8
- frequency: float32 [4096], P('comp'), may hold values from 0.5 to 8
- amplitude: float32 [3, 4096], P(None, 'comp'), may hold values from -0.09375 to 0.09375
- phase_index: int32 [4096], P('comp'), may hold values from 0 to 255
- phase_table: float32 [256], replicated, may hold values from -3.140625 to 3.140625
Outputs:
- final_field: float32 [3, 256, 64, 256], P(None, 'slab', 'comp')
- prior_field: float32 [3, 256, 64, 256], P(None, 'slab', 'comp')
Inputs may be any that keep to these rules, and one draw needn't show every extreme that they name: `point_owner`: the device at position s of slab and c of comp is numbered s times the size of comp plus c. Among the rows of one device at most 16 points name one owner.
All inputs are finite; a program needn't handle non-finite values.
Results may differ from a plain program's by a relative error of at most 0.0003.
Values sent between devices are 32-bit elements; how exact they have to be, the bound alone decides.
A program may use at most 192 MiB of HBM per device.

v0:
```python
import jax
import jax.numpy as jnp
from jax import lax
from jax.sharding import PartitionSpec as P

STEPS = 3


step_size = 0.05
near_weight = 4.0 / 3.0
far_weight = -1.0 / 12.0
centre_weight = -7.5


def with_halo(block, sides, width):
    for axis, dim in sides:
        count = lax.axis_size(axis)
        forward = [(i, i + 1) for i in range(count - 1)]
        backward = [(target, source) for source, target in forward]
        low = lax.ppermute(
            lax.slice_in_dim(block, block.shape[dim] - width, None, axis=dim), axis, forward
        )
        high = lax.ppermute(lax.slice_in_dim(block, 0, width, axis=dim), axis, backward)
        block = jnp.concatenate([low, block, high], axis=dim)
    return block


def shifted(padded, axis_pos, offset):
    result = padded
    for dim_pos in (1, 2, 3):
        first_cell = 2 + offset if dim_pos == axis_pos else 2
        result = lax.slice_in_dim(
            result, first_cell, first_cell + padded.shape[dim_pos] - 4, axis=dim_pos
        )
    return result


def laplace_four(padded):
    summed = centre_weight * shifted(padded, 0, 0)
    for axis_pos in (1, 2, 3):
        summed = summed + near_weight * (
            shifted(padded, axis_pos, 1) + shifted(padded, axis_pos, -1)
        )
        summed = summed + far_weight * (
            shifted(padded, axis_pos, 2) + shifted(padded, axis_pos, -2)
        )
    return summed


def incident_terms(comp_block, coords):
    angles = (
        comp_block[0][:, None] * coords[0][None, :]
        + comp_block[1][:, None] * coords[1][None, :]
        + comp_block[2][:, None] * coords[2][None, :]
    )
    cosine = jnp.cos(angles)
    sine_part = jnp.sin(angles)
    moments = step_size * (jnp.arange(STEPS) + 1).astype(jnp.float32)
    delays = moments[:, None] * comp_block[3][None, :] - comp_block[7][None, :]
    block_width = comp_block.shape[1]
    left_cos = (jnp.cos(delays)[:, None, :] * comp_block[4:7][None, :, :]).reshape(
        STEPS * 3, block_width
    )
    left_sin = (jnp.sin(delays)[:, None, :] * comp_block[4:7][None, :, :]).reshape(
        STEPS * 3, block_width
    )
    first_part = jnp.dot(
        left_cos, cosine, precision=lax.Precision.HIGHEST, preferred_element_type=jnp.float32
    )
    second_part = jnp.dot(
        left_sin, sine_part, precision=lax.Precision.HIGHEST, preferred_element_type=jnp.float32
    )
    return first_part + second_part


def local(
    current_field,
    earlier_field,
    wave_coef,
    layer_mask,
    point_xyz,
    point_owner,
    cell_offset,
    wave_vector,
    frequency,
    amplitude,
    phase_index,
    phase_table,
):
    table_size = phase_table.shape[0]
    matches = (phase_index[None, :] == jnp.arange(table_size)[:, None]).astype(jnp.float32)
    phases = jnp.dot(
        phase_table[None, :],
        matches,
        precision=lax.Precision.HIGHEST,
        preferred_element_type=jnp.float32,
    )[0]
    own_block = jnp.concatenate(
        [wave_vector, frequency[None, :], amplitude, phases[None, :]], axis=0
    )
    point_count = point_xyz.shape[1]
    slab_count = lax.axis_size("slab")
    comp_count = lax.axis_size("comp")
    device_count = slab_count * comp_count
    slot_count = max(2, 2 * point_count // device_count)
    rows_out = STEPS * 3
    incident = incident_terms(lax.all_gather(own_block, "comp", axis=1, tiled=True), point_xyz)
    owners = point_owner[:, 0]
    matched = (owners[:, None] == jnp.arange(device_count)[None, :]).astype(jnp.int32)
    ranking = jnp.sum((jnp.cumsum(matched, axis=0) - 1) * matched, axis=1)
    value_index = (
        owners[None, :] * (rows_out * slot_count)
        + jnp.arange(rows_out)[:, None] * slot_count
        + ranking[None, :]
    )
    value_buffer = (
        jnp.zeros((device_count * rows_out * slot_count,), jnp.float32)
        .at[value_index.reshape(-1)]
        .set(incident.reshape(-1))
    )
    offset_buffer = (
        jnp.zeros((device_count * slot_count,), jnp.int32)
        .at[owners * slot_count + ranking]
        .set(cell_offset)
    )
    got_values, got_offsets = (
        lax.all_to_all(
            value_buffer.reshape(device_count, rows_out * slot_count),
            ("slab", "comp"),
            split_axis=0,
            concat_axis=0,
            tiled=True,
        ),
        lax.all_to_all(
            offset_buffer.reshape(device_count, slot_count),
            ("slab", "comp"),
            split_axis=0,
            concat_axis=0,
            tiled=True,
        ),
    )
    arrived = jnp.transpose(
        got_values.reshape(device_count, rows_out, slot_count), (1, 0, 2)
    ).reshape(rows_out, device_count * slot_count)
    cell_count = current_field.shape[1] * current_field.shape[2] * current_field.shape[3]
    forcing = (
        jnp.zeros((rows_out, cell_count), jnp.float32).at[:, got_offsets.reshape(-1)].add(arrived)
    )
    sign_field = ((layer_mask == 1).astype(jnp.float32) - (layer_mask == 2).astype(jnp.float32))[
        None
    ]
    current = current_field
    earlier = earlier_field
    for step_index in range(STEPS):
        widened = with_halo(current, (("slab", 1), ("comp", 2)), 2)
        padded = jnp.pad(widened, ((0, 0), (0, 0), (0, 0), (2, 2)))
        source = forcing[3 * step_index : 3 * step_index + 3].reshape(current.shape)
        following = (
            2.0 * current - earlier + wave_coef[None] * laplace_four(padded) + sign_field * source
        )
        earlier = current
        current = following
    return (current, earlier)


def solution(mesh):
    in_specs = (
        P(None, "slab", "comp", None),
        P(None, "slab", "comp", None),
        P("slab", "comp", None),
        P("slab", "comp", None),
        P(None, ("slab", "comp")),
        P(("slab", "comp"), None),
        P(("slab", "comp")),
        P(None, "comp"),
        P("comp"),
        P(None, "comp"),
        P("comp"),
        P(),
    )
    out_specs = (P(None, "slab", "comp", None), P(None, "slab", "comp", None))
    return jax.shard_map(local, mesh=mesh, in_specs=in_specs, out_specs=out_specs, check_vma=False)
```

profile of v0, /device:TPU:9, one launch (start us, length us, event | category | flops | bytes accessed | tf_op | source)
XLA Modules:
  0.0 364.1 jit_solution(6229972985461683662)
XLA Ops:
  0.6 0.0 copy-start
  0.6 0.8 copy.32
  1.4 0.2 fusion.25
  1.8 0.0 copy-start.9
  1.8 0.0 copy-start.11
  1.8 0.1 copy.33
  1.9 0.2 copy-done.7
  2.1 0.4 fusion.23
  2.5 4.5 %scatter_custom_fusion = s32[2048]{0:T(1024)S(1)} fusion(s32[1024]{0:T(1024)S(1)} %bitcast.65, s32[1024]{0:T(1024)} %param.18, s32[]{:T(128)} %constant.5.clone.1), kind=kCustom, calls=%fused_computation.167 | custom fusion | bytes 8704 | tf_op jit(solution)/shard_map/scatter | solution.py:124
  7.0 0.7 all_to_all.12
  7.7 10.8 %all-to-all-start = ((s32[128,1,16]{2,1,0:T(1,128)}), s32[128,1,16]{2,1,0:T(1,128)S(1)}, u32[]{:S(2)}, u32[]{:S(2)}) async-start(s32[128,1,16]{2,1,0:T(1,128)} %bitcast.7), calls=%async_computation | async-start | bytes 131072 | tf_op jit(solution)/shard_map/all_to_all | solution.py:134
  18.5 3.1 collective-permute-start.1
  21.6 6.7 %collective-permute-start = (f32[3,2,16,256]{3,2,1,0:T(8,128)S(1)}, f32[3,2,16,256]{3,2,1,0:T(8,128)S(1)}, u32[]{:S(2)}, u32[]{:S(2)}) collective-permute-start(f32[3,2,16,256]{3,2,1,0:T(8,128)S(1)} %get-tuple-element.18), channel_id=1, source_target_pairs={{4,0},{8,4},{12,8},{16,12},{20,16},{24,20},{28,24},{32,28},{36,32}... | collective-permute-start | bytes 294920 | tf_op jit(solution)/shard_map/ppermute | solution.py:23
  28.4 0.4 fusion.22
  28.8 6.2 %all_gather.3 = f32[8,4096]{1,0:T(8,128)S(1)} all-gather(f32[8,1024]{1,0:T(8,128)S(1)} %pad_maximum_fusion.24), channel_id=1, replica_groups=mesh['slab'=32,'comp'=4] {'comp'}, dimensions={1}, use_global_device_ids=true | all-gather | bytes 163840 | tf_op jit(solution)/shard_map/all_gather | solution.py:107
  35.0 0.1 fusion.95
  35.1 0.5 fusion.85
  35.7 0.1 broadcast_multiply_fusion.1
  35.8 0.1 mul.296
  35.9 0.1 mul.278
  35.9 0.1 add_bitcast_fusion
  36.1 77.3 %fusion = f32[9,1024]{1,0:T(8,128)S(1)} fusion(f32[9,4096]{1,0:T(8,128)S(1)} %mul.296, f32[1024]{0:T(1024)S(1)} %bitcast.68, f32[4096]{0:T(1024)S(1)} %bitcast.59, f32[1024]{0:T(1024)S(1)} %bitcast.70, f32[4096]{0:T(1024)S(1)} %bitcast.61, f32[1024]{0:T(1024)S(1)} %bitcast.66, f32[4096]{0:T(1024)S(1)} %bitcast.57), kind=kOutput, calls=%fused_computation.3 | convolution fusion | flops 473956352 | bytes 245760 | tf_op jit(solution)/shard_map/dot_general | solution.py:70
  113.4 65.0 %fusion.19 = f32[9,1024]{1,0:T(8,128)S(1)} fusion(f32[9,1024]{1,0:T(8,128)S(1)} %fusion, f32[9,4096]{1,0:T(8,128)S(1)} %mul.278, f32[1024]{0:T(1024)S(1)} %bitcast.69, f32[4096]{0:T(1024)S(1)} %bitcast.60, f32[1024]{0:T(1024)S(1)} %bitcast.71, f32[4096]{0:T(1024)S(1)} %bitcast.62, f32[1024]{0:T(1024)S(1)} %bitcast.67, f32[4096]{0:T(1024)S(1)} %bitcast.58), kind=kOutput, calls=%fused_computation.35 | convolution fusion | flops 473965568 | bytes 282624 | tf_op jit(solution)/shard_map/dot_general | solution.py:67
  178.4 34.2 %scatter_custom_fusion.1 = f32[18432]{0:T(1024)S(1)} fusion(s32[9216]{0:T(1024)S(1)} %bitcast.56, f32[9216]{0:T(1024)S(1)} %reshape.255, f32[]{:T(128)} %constant.19.clone.1), kind=kCustom, calls=%fused_computation.155 | custom fusion | bytes 73732 | tf_op jit(solution)/shard_map/scatter | solution.py:119
  212.7 0.9 all_to_all.16
  213.6 6.7 %all-to-all-start.1 = ((f32[128,1,144]{2,1,0:T(1,128)}), f32[128,1,144]{2,1,0:T(1,128)S(1)}, u32[]{:S(2)}, u32[]{:S(2)}) async-start(f32[128,1,144]{2,1,0:T(1,128)} %all_to_all.16), calls=%async_computation.1 | async-start | bytes 262144 | tf_op jit(solution)/shard_map/all_to_all | solution.py:127
  220.3 0.5 broadcast.239
  220.8 0.8 reduce.3
  221.6 0.1 reshape.236
  221.7 7.7 %all-to-all-done.1 = f32[128,1,144]{2,1,0:T(1,128)S(1)} async-done(((f32[128,1,144]{2,1,0:T(1,128)}), f32[128,1,144]{2,1,0:T(1,128)S(1)}, u32[]{:S(2)}, u32[]{:S(2)}) %all-to-all-start.1) | async-done | bytes 73760 | tf_op jit(solution)/shard_map/all_to_all | solution.py:127
  229.5 0.1 copy.36
  229.6 0.2 copy.37
  229.8 0.3 reshape.260
  230.1 0.4 copy.38
  230.5 18.4 %scatter_custom_fusion.2 = f32[9,32768]{0,1:T(8,128)} fusion(s32[2048]{0:T(1024)S(1)} %bitcast.63, f32[2048,9]{1,0:T(8,128)S(1)} %copy.38, f32[]{:T(128)} %constant.19.clone.1), kind=kCustom, calls=%fused_computation.20 | custom fusion | flops 18432 | bytes 1179652 | tf_op jit(solution)/shard_map/scatter-add | solution.py:147
  248.9 0.1 constant_dynamic-update-slice_fusion.1
  249.1 0.1 fusion.91
  249.2 2.2 collective-permute-start.2
  251.4 3.4 collective-permute-start.3
  254.7 34.7 %fusion.90 = (f32[3,32768]{0,1:T(8,128)}, f32[3,32768]{0,1:T(8,128)}, f32[3,32768]{0,1:T(8,128)}) fusion(f32[9,32768]{0,1:T(8,128)} %scatter_custom_fusion.2), kind=kLoop, calls=%fused_computation.172 | loop fusion | bytes 2359296 | tf_op jit(solution)/shard_map/slice | solution.py:157
  289.5 10.0 %copy.39 = f32[3,8,16,256]{3,2,1,0:T(8,128)S(1)} copy(f32[3,8,16,256]{0,3,2,1:T(8,128)} %bitcast.46) | data formatting | bytes 786432 | tf_op jit(solution)/shard_map/reshape | solution.py:157
  299.5 0.7 select_maximum_fusion.8
  300.2 0.2 copy-done.4
  300.4 0.2 copy-done.5
  300.5 0.6 fusion.71
  301.2 4.6 %collective-permute-start.4 = (f32[3,2,16,256]{3,2,1,0:T(8,128)S(1)}, f32[3,2,16,256]{3,2,1,0:T(8,128)S(1)}, u32[]{:S(2)}, u32[]{:S(2)}) collective-permute-start(f32[3,2,16,256]{3,2,1,0:T(8,128)S(1)} %get-tuple-element.13), channel_id=1, source_target_pairs={{4,0},{8,4},{12,8},{16,12},{20,16},{24,20},{28,24},{32,28},{36,32}... | collective-permute-start | bytes 294920 | tf_op jit(solution)/shard_map/ppermute | solution.py:23
  305.8 1.9 collective-permute-start.5
  307.7 8.5 %collective-permute-done.5 = f32[3,2,16,256]{3,2,1,0:T(8,128)S(1)} collective-permute-done((f32[3,2,16,256]{3,2,1,0:T(8,128)S(1)}, f32[3,2,16,256]{3,2,1,0:T(8,128)S(1)}, u32[]{:S(2)}, u32[]{:S(2)}) %collective-permute-start.5) | collective-permute-done | bytes 98336 | tf_op jit(solution)/shard_map/ppermute | solution.py:20
  316.2 0.1 pad_maximum_fusion.21
  316.3 2.2 collective-permute-start.6
  318.5 3.4 collective-permute-start.7
  321.9 10.2 %copy.40 = f32[3,8,16,256]{3,2,1,0:T(8,128)S(1)} copy(f32[3,8,16,256]{0,3,2,1:T(8,128)} %bitcast.45) | data formatting | bytes 786432 | tf_op jit(solution)/shard_map/reshape | solution.py:157
  332.1 0.7 select_maximum_fusion.4
  332.8 0.7 fusion.51
  333.5 1.9 collective-permute-start.8
  335.5 3.4 collective-permute-start.9
  338.8 0.6 collective-permute-done.8
  339.5 6.4 %collective-permute-done.9 = f32[3,2,16,256]{3,2,1,0:T(8,128)S(1)} collective-permute-done((f32[3,2,16,256]{3,2,1,0:T(8,128)S(1)}, f32[3,2,16,256]{3,2,1,0:T(8,128)S(1)}, u32[]{:S(2)}, u32[]{:S(2)}) %collective-permute-start.9) | collective-permute-done | bytes 98336 | tf_op jit(solution)/shard_map/ppermute | solution.py:20
  345.9 0.1 pad_maximum_fusion.18
  346.0 2.2 collective-permute-start.10
  348.1 3.4 collective-permute-start.11
  351.5 10.0 %copy.41 = f32[3,8,16,256]{3,2,1,0:T(8,128)S(1)} copy(f32[3,8,16,256]{0,3,2,1:T(8,128)} %bitcast.44) | data formatting | bytes 786432 | tf_op jit(solution)/shard_map/reshape | solution.py:157
  361.5 0.7 select_maximum_fusion
  362.3 1.4 fusion.38
  (51 shorter events, 0.4 us)
Async XLA Ops:
  0.6 27.7 %copy-start = (f32[256]{0:T(256)S(1)}, f32[256]{0:T(256)}, u32[]{:S(2)}) copy-start(f32[256]{0:T(256)} %param.23) | copy-start | bytes 3076
  1.4 0.7 copy-start.7
  1.7 16.8 %copy-start.3 = (f32[3,8,16,256]{3,2,1,0:T(8,128)S(1)}, f32[3,8,16,256]{3,2,1,0:T(8,128)}, u32[]{:S(2)}) copy-start(f32[3,8,16,256]{3,2,1,0:T(8,128)} %param.12) | copy-start | bytes 1179652
  1.8 26.6 %copy-start.12 = (s32[1024]{0:T(1024)S(1)}, s32[1024]{0:T(1024)}, u32[]{:S(2)}) copy-start(s32[1024]{0:T(1024)} %param.22) | copy-start | bytes 12292
  1.8 27.0 %copy-start.8 = (f32[3,1024]{1,0:T(4,128)S(1)}, f32[3,1024]{1,0:T(4,128)}, u32[]{:S(2)}) copy-start(f32[3,1024]{1,0:T(4,128)} %param.21) | copy-start | bytes 36868
  1.8 27.0 %copy-start.9 = (f32[3,1024]{1,0:T(4,128)S(1)}, f32[3,1024]{1,0:T(4,128)}, u32[]{:S(2)}) copy-start(f32[3,1024]{1,0:T(4,128)} %param.19) | copy-start | bytes 36868
  1.8 27.0 %copy-start.11 = (f32[1024]{0:T(1024)S(1)}, f32[1024]{0:T(1024)}, u32[]{:S(2)}) copy-start(f32[1024]{0:T(1024)} %param.20) | copy-start | bytes 12292
  2.5 33.3 %copy-start.10 = (f32[3,1024]{1,0:T(4,128)S(1)}, f32[3,1024]{1,0:T(4,128)}, u32[]{:S(2)}) copy-start(f32[3,1024]{1,0:T(4,128)} %param.16) | copy-start | bytes 36868
  7.7 205.9 %all-to-all-start = ((s32[128,1,16]{2,1,0:T(1,128)}), s32[128,1,16]{2,1,0:T(1,128)S(1)}, u32[]{:S(2)}, u32[]{:S(2)}) async-start(s32[128,1,16]{2,1,0:T(1,128)} %bitcast.7), calls=%async_computation | async-start | bytes 131072 | tf_op jit(solution)/shard_map/all_to_all | solution.py:134
  18.5 230.4 %collective-permute-start.1 = (f32[3,2,16,256]{3,2,1,0:T(8,128)S(1)}, f32[3,2,16,256]{3,2,1,0:T(8,128)S(1)}, u32[]{:S(2)}, u32[]{:S(2)}) collective-permute-start(f32[3,2,16,256]{3,2,1,0:T(8,128)S(1)} %get-tuple-element.19), channel_id=1, source_target_pairs={{0,4},{4,8},{8,12},{12,16},{16,20},{20,24},{24,28},{28,32},{32,36}... | collective-permute-start | bytes 294920 | tf_op jit(solution)/shard_map/ppermute | solution.py:20
  21.6 227.5 %collective-permute-start = (f32[3,2,16,256]{3,2,1,0:T(8,128)S(1)}, f32[3,2,16,256]{3,2,1,0:T(8,128)S(1)}, u32[]{:S(2)}, u32[]{:S(2)}) collective-permute-start(f32[3,2,16,256]{3,2,1,0:T(8,128)S(1)} %get-tuple-element.18), channel_id=1, source_target_pairs={{4,0},{8,4},{12,8},{16,12},{20,16},{24,20},{28,24},{32,28},{36,32}... | collective-permute-start | bytes 294920 | tf_op jit(solution)/shard_map/ppermute | solution.py:23
  113.4 65.0 %copy-start.6 = (s32[8,16,256]{2,1,0:T(8,128)S(1)}, s32[8,16,256]{2,1,0:T(8,128)}, u32[]{:S(2)}) copy-start(s32[8,16,256]{2,1,0:T(8,128)} %param.15) | copy-start | bytes 393220
  213.6 15.9 %all-to-all-start.1 = ((f32[128,1,144]{2,1,0:T(1,128)}), f32[128,1,144]{2,1,0:T(1,128)S(1)}, u32[]{:S(2)}, u32[]{:S(2)}) async-start(f32[128,1,144]{2,1,0:T(1,128)} %all_to_all.16), calls=%async_computation.1 | async-start | bytes 262144 | tf_op jit(solution)/shard_map/all_to_all | solution.py:127
  249.2 50.3 %collective-permute-start.2 = (f32[3,12,2,256]{3,2,1,0:T(2,128)S(1)}, f32[3,12,2,256]{3,2,1,0:T(2,128)S(1)}, u32[]{:S(2)}, u32[]{:S(2)}) collective-permute-start(f32[3,12,2,256]{3,2,1,0:T(2,128)S(1)} %get-tuple-element.10), channel_id=1, source_target_pairs={{1,0},{2,1},{3,2},{5,4},{6,5},{7,6},{9,8},{10,9},{11,10},{13,12},{... | collective-permute-start | bytes 221192 | tf_op jit(solution)/shard_map/ppermute | solution.py:23
  251.4 48.1 %collective-permute-start.3 = (f32[3,12,2,256]{3,2,1,0:T(2,128)S(1)}, f32[3,12,2,256]{3,2,1,0:T(2,128)S(1)}, u32[]{:S(2)}, u32[]{:S(2)}) collective-permute-start(f32[3,12,2,256]{3,2,1,0:T(2,128)S(1)} %get-tuple-element.9), channel_id=1, source_target_pairs={{0,1},{1,2},{2,3},{4,5},{5,6},{6,7},{8,9},{9,10},{10,11},{12,13},{... | collective-permute-start | bytes 221192 | tf_op jit(solution)/shard_map/ppermute | solution.py:20
  299.4 0.9 copy-start.4
  299.5 1.1 copy-start.5
  301.2 6.5 %collective-permute-start.4 = (f32[3,2,16,256]{3,2,1,0:T(8,128)S(1)}, f32[3,2,16,256]{3,2,1,0:T(8,128)S(1)}, u32[]{:S(2)}, u32[]{:S(2)}) collective-permute-start(f32[3,2,16,256]{3,2,1,0:T(8,128)S(1)} %get-tuple-element.13), channel_id=1, source_target_pairs={{4,0},{8,4},{12,8},{16,12},{20,16},{24,20},{28,24},{32,28},{36,32}... | collective-permute-start | bytes 294920 | tf_op jit(solution)/shard_map/ppermute | solution.py:23
  305.8 10.4 %collective-permute-start.5 = (f32[3,2,16,256]{3,2,1,0:T(8,128)S(1)}, f32[3,2,16,256]{3,2,1,0:T(8,128)S(1)}, u32[]{:S(2)}, u32[]{:S(2)}) collective-permute-start(f32[3,2,16,256]{3,2,1,0:T(8,128)S(1)} %get-tuple-element.14), channel_id=1, source_target_pairs={{0,4},{4,8},{8,12},{12,16},{16,20},{20,24},{24,28},{28,32},{32,36}... | collective-permute-start | bytes 294920 | tf_op jit(solution)/shard_map/ppermute | solution.py:20
  316.3 15.8 %collective-permute-start.6 = (f32[3,12,2,256]{3,2,1,0:T(2,128)S(1)}, f32[3,12,2,256]{3,2,1,0:T(2,128)S(1)}, u32[]{:S(2)}, u32[]{:S(2)}) collective-permute-start(f32[3,12,2,256]{3,2,1,0:T(2,128)S(1)} %get-tuple-element.8), channel_id=1, source_target_pairs={{1,0},{2,1},{3,2},{5,4},{6,5},{7,6},{9,8},{10,9},{11,10},{13,12},{... | collective-permute-start | bytes 221192 | tf_op jit(solution)/shard_map/ppermute | solution.py:23
  318.5 13.6 %collective-permute-start.7 = (f32[3,12,2,256]{3,2,1,0:T(2,128)S(1)}, f32[3,12,2,256]{3,2,1,0:T(2,128)S(1)}, u32[]{:S(2)}, u32[]{:S(2)}) collective-permute-start(f32[3,12,2,256]{3,2,1,0:T(2,128)S(1)} %get-tuple-element.7), channel_id=1, source_target_pairs={{0,1},{1,2},{2,3},{4,5},{5,6},{6,7},{8,9},{9,10},{10,11},{12,13},{... | collective-permute-start | bytes 221192 | tf_op jit(solution)/shard_map/ppermute | solution.py:20
  333.5 28.8 %copy-start.2 = (f32[3,8,16,256]{3,2,1,0:T(8,128)}, f32[3,8,16,256]{3,2,1,0:T(8,128)S(1)}, u32[]{:S(2)}) copy-start(f32[3,8,16,256]{3,2,1,0:T(8,128)S(1)} %fusion.51) | copy-start | bytes 1179652
  333.5 5.9 %collective-permute-start.8 = (f32[3,2,16,256]{3,2,1,0:T(8,128)S(1)}, f32[3,2,16,256]{3,2,1,0:T(8,128)S(1)}, u32[]{:S(2)}, u32[]{:S(2)}) collective-permute-start(f32[3,2,16,256]{3,2,1,0:T(8,128)S(1)} %get-tuple-element.11), channel_id=1, source_target_pairs={{4,0},{8,4},{12,8},{16,12},{20,16},{24,20},{28,24},{32,28},{36,32}... | collective-permute-start | bytes 294920 | tf_op jit(solution)/shard_map/ppermute | solution.py:23
  335.5 10.4 %collective-permute-start.9 = (f32[3,2,16,256]{3,2,1,0:T(8,128)S(1)}, f32[3,2,16,256]{3,2,1,0:T(8,128)S(1)}, u32[]{:S(2)}, u32[]{:S(2)}) collective-permute-start(f32[3,2,16,256]{3,2,1,0:T(8,128)S(1)} %get-tuple-element.12), channel_id=1, source_target_pairs={{0,4},{4,8},{8,12},{12,16},{16,20},{20,24},{24,28},{28,32},{32,36}... | collective-permute-start | bytes 294920 | tf_op jit(solution)/shard_map/ppermute | solution.py:20
  346.0 15.6 %collective-permute-start.10 = (f32[3,12,2,256]{3,2,1,0:T(2,128)S(1)}, f32[3,12,2,256]{3,2,1,0:T(2,128)S(1)}, u32[]{:S(2)}, u32[]{:S(2)}) collective-permute-start(f32[3,12,2,256]{3,2,1,0:T(2,128)S(1)} %get-tuple-element.6), channel_id=1, source_target_pairs={{1,0},{2,1},{3,2},{5,4},{6,5},{7,6},{9,8},{10,9},{11,10},{13,12},{... | collective-permute-start | bytes 221192 | tf_op jit(solution)/shard_map/ppermute | solution.py:23
  348.1 13.4 %collective-permute-start.11 = (f32[3,12,2,256]{3,2,1,0:T(2,128)S(1)}, f32[3,12,2,256]{3,2,1,0:T(2,128)S(1)}, u32[]{:S(2)}, u32[]{:S(2)}) collective-permute-start(f32[3,12,2,256]{3,2,1,0:T(2,128)S(1)} %get-tuple-element.5), channel_id=1, source_target_pairs={{0,1},{1,2},{2,3},{4,5},{5,6},{6,7},{8,9},{9,10},{10,11},{12,13},{... | collective-permute-start | bytes 221192 | tf_op jit(solution)/shard_map/ppermute | solution.py:20
  361.5 2.2 copy-start.1
where the time goes:
time: 369 us; the launch traced here: 364 us
  matrix products  143 us (39%)
  local copies, waits for them, and re-layouts  109 us (30%)
  starting transfers between devices  55.7 us (15%)
  other arithmetic  25.6 us (7%)
  waiting for transfers between devices  23.3 us (6%)
  blocking collectives  6.18 us (2%)
    dot_general x1, matrix products, incident_terms(): jnp.dot(left_sin, sine_part, precision=lax.Precision.HIGHEST, preferred_e...  77.3 us
    dot_general x1, matrix products, incident_terms(): jnp.dot(left_cos, cosine, precision=lax.Precision.HIGHEST, preferred_elem...  65 us
    slice x1, local copies, waits for them, and re-layouts, local(): source = forcing[3 * step_index:3 * step_index + 3].reshape(current.shape)  34.7 us
    scatter x1, local copies, waits for them, and re-layouts, local(): value_buffer = jnp.zeros((device_count * rows_out * slot_count,), jnp.flo...  34.2 us
    reshape x3, local copies, waits for them, and re-layouts, local(): source = forcing[3 * step_index:3 * step_index + 3].reshape(current.shape)  30.2 us
    ppermute x6, starting transfers between devices, with_halo(): lax.ppermute(lax.slice_in_dim(block, 0, width, axis=dim), axis, backward)  19.8 us
    ppermute x6, starting transfers between devices, with_halo(): lax.ppermute(lax.slice_in_dim(block, block.shape[dim] - width, None, axis...  18.5 us
    scatter-add x1, other arithmetic, local(): jnp.zeros((rows_out, cell_count), jnp.float32)  18.4 us
  transfers between devices with their start and end apart: 14, of which 4 were waited for; matrix products, arithmetic and copies ran while one was open for 72% of the time, Pallas kernels for 0%

commit v1 on v0

v1 whole, which is shorter than its diff:
```python
import functools

import jax
import jax.numpy as jnp
import numpy as np
from jax import lax
from jax.experimental import pallas as pl
from jax.experimental.pallas import tpu as pltpu
from jax.sharding import PartitionSpec as P

STEPS = 3
SLOTS = 16
HALF = 16
MODES = 2 * HALF
FIELDS = 9
F32 = jnp.float32
BF16 = jnp.bfloat16

step_size = 0.05
near_weight = 4.0 / 3.0
far_weight = -1.0 / 12.0
centre_weight = -7.5


def turn_series(degree):
    fits = []
    for h in (
        lambda s: np.cos(2 * np.pi * np.sqrt(s)),
        lambda s: np.sinc(2 * np.sqrt(s)) * 2 * np.pi,
    ):
        fit = np.polynomial.chebyshev.Chebyshev.interpolate(h, degree, domain=[0, 0.25])
        fits.append([float(c) for c in fit.convert(kind=np.polynomial.Polynomial).coef])
    return fits


COS_SERIES, SIN_SERIES = turn_series(7)


def horner(series, s):
    total = jnp.full_like(s, series[-1])
    for c in series[-2::-1]:
        total = total * s + c
    return total


def cos_sin_turns(u):
    r = u - jnp.round(u)
    s = r * r
    return horner(COS_SERIES, s), r * horner(SIN_SERIES, s)


def mode_tables():
    a = np.arange(HALF)
    angle = (2 * a + 1) * np.pi / (2 * MODES)
    nodes = np.cos(angle)
    weight = np.zeros((6 * HALF, 6 * HALF))
    for dim in range(3):
        for parity in (0, 1):
            m = 2 * np.arange(HALF) + parity
            block = 4.0 / MODES * np.cos(m[:, None] * angle[None, :])
            if parity == 0:
                block[0] *= 0.5
            at = (parity * 3 + dim) * HALF
            weight[at : at + HALF, at : at + HALF] = block
    column = np.tile(nodes, 3)[:, None] * np.ones((1, 128))
    return weight.astype(np.float32), column.astype(np.float32)


def split2(x):
    high = x.astype(BF16)
    return high, (x - high.astype(F32)).astype(BF16)


def dot_nt(a, b):
    return lax.dot_general(a, b, (((1,), (1,)), ((), ())), preferred_element_type=F32)


def dot_nn(a, b):
    return lax.dot_general(a, b, (((1,), (0,)), ((), ())), preferred_element_type=F32)


def pack_kernel(owner_ref, xyz_ref, offset_ref, wave_ref, freq_ref, amp_ref, index_ref, table_ref, send_ref, comp_ref):
    points = owner_ref.shape[1]
    devices = send_ref.shape[0]
    hit = owner_ref[...] == lax.broadcasted_iota(jnp.int32, (devices, points), 0)
    match = jnp.where(hit, 1.0, 0.0)
    match16 = match.astype(BF16)
    before = (
        lax.broadcasted_iota(jnp.int32, (points, points), 0)
        < lax.broadcasted_iota(jnp.int32, (points, points), 1)
    )
    count = dot_nn(match16, jnp.where(before, 1.0, 0.0).astype(BF16))
    rank = jnp.sum(count * match, axis=0, keepdims=True)
    slot = rank == lax.broadcasted_iota(jnp.int32, (SLOTS, points), 0).astype(F32)
    values = [xyz_ref[i : i + 1, :] for i in range(3)] + [(offset_ref[...] + 1).astype(F32)]
    spread = jnp.concatenate([jnp.where(slot, v, 0.0) for v in values], axis=0)
    first, rest = split2(spread)
    rest = spread - first.astype(F32)
    second, third = split2(rest)
    send_ref[...] = dot_nt(match16, first) + dot_nt(match16, second) + dot_nt(match16, third)
    entries = table_ref.shape[0]
    found = index_ref[...] == lax.broadcasted_iota(jnp.int32, (entries, index_ref.shape[1]), 0)
    phase = jnp.sum(jnp.where(found, table_ref[...], 0.0), axis=0, keepdims=True)
    comp_ref[0:3, :] = wave_ref[...]
    comp_ref[3:4, :] = freq_ref[...]
    comp_ref[4:7, :] = amp_ref[...]
    comp_ref[7:8, :] = phase


def mode_sums(block, weight, column, q_hi, q_lo, p_hi, p_lo):
    width = block.shape[1]
    turn = 1.0 / (2.0 * np.pi)
    angles = jnp.concatenate(
        [column[d * HALF : (d + 1) * HALF, 0:1] * (block[d : d + 1, :] * (2.0 * turn)) for d in range(3)], axis=0
    )
    cosine, sine = cos_sin_turns(angles)
    series = lax.dot_general(
        weight, jnp.concatenate([cosine, sine], axis=0), (((1,), (0,)), ((), ())),
        precision=lax.Precision.HIGHEST, preferred_element_type=F32,
    )
    cx, cy, cz, sx, sy, sz = [series[i * HALF : (i + 1) * HALF, :] for i in range(6)]
    centre = (2.0 * turn) * (block[0:1, :] + block[1:2, :] + block[2:3, :]) + turn * block[7:8, :]
    for n in range(STEPS):
        shift_cos, shift_sin = cos_sin_turns(centre - block[3:4, :] * (turn * step_size * (n + 1)))
        for i in range(3):
            b = block[4 + i : 5 + i, :] * shift_cos
            c = -block[4 + i : 5 + i, :] * shift_sin
            at = (3 * n + i) * MODES
            for which, part, value in ((0, 0, b * cz), (0, 1, c * sz), (1, 0, c * cz), (1, 1, -(b * sz))):
                rows = pl.ds(at + part * HALF, HALF)
                q_hi[which, rows, :], q_lo[which, rows, :] = split2(value)
    for m in range(HALF):
        rows_a, rows_b = pl.ds(m * HALF, HALF), pl.ds((HALF + m) * HALF, HALF)
        x_even, x_odd = cx[m : m + 1, :], sx[m : m + 1, :]
        p_hi[0, rows_a, :], p_lo[0, rows_a, :] = split2(x_even * cy)
        p_hi[0, rows_b, :], p_lo[0, rows_b, :] = split2(-(x_odd * sy))
        p_hi[1, rows_a, :], p_lo[1, rows_a, :] = split2(x_even * sy)
        p_hi[1, rows_b, :], p_lo[1, rows_b, :] = split2(x_odd * cy)


def mode_products(q_hi, q_lo, p_hi, p_lo, which):
    return (
        dot_nt(q_hi[which], p_hi[which]) + dot_nt(q_hi[which], p_lo[which]) + dot_nt(q_lo[which], p_hi[which])
    )


def slot_rows(arrived):
    turned = arrived.T
    return [
        jnp.concatenate([turned[c * SLOTS + r : c * SLOTS + r + 1, :] for r in range(SLOTS)], axis=1)
        for c in range(4)
    ]


def point_modes(rows, t_ref):
    tau = jnp.concatenate([(r - 2.0) * 0.5 for r in rows], axis=0)
    older, old = jnp.ones_like(tau), tau
    for m in range(MODES):
        at = (m % 2) * HALF + m // 2
        for d in range(3):
            t_ref[d, at : at + 1, :] = older[d : d + 1, :]
        older, old = old, 2.0 * tau * old - older


def point_sums(t_ref, lanes, f_hi, f_lo, w_hi, w_lo, v_ref):
    tx, ty, tz = t_ref[0, :, lanes], t_ref[1, :, lanes], t_ref[2, :, lanes]
    half = [slice(0, HALF), slice(HALF, MODES)]
    for combo, (px, py) in enumerate(((0, 0), (1, 1), (0, 1), (1, 0))):
        other = ty[half[py], :]
        for m in range(HALF):
            rows = pl.ds((combo * HALF + m) * HALF, HALF)
            at = px * HALF + m
            w_hi[rows, :], w_lo[rows, :] = split2(tx[at : at + 1, :] * other)
    sums = dot_nn(f_hi[...], w_hi[...]) + dot_nn(f_hi[...], w_lo[...]) + dot_nn(f_lo[...], w_hi[...])
    for j in range(FIELDS):
        v_ref[j : j + 1, lanes] = jnp.sum(sums[j * MODES : (j + 1) * MODES, :] * tz, axis=0, keepdims=True)


def spread_field(v, place, z_hot, cells_xy):
    hit = place == lax.broadcasted_iota(jnp.int32, (cells_xy, place.shape[1]), 0).astype(F32)
    v_hi, v_lo = split2(jnp.where(hit, v, 0.0))
    return dot_nt(v_hi, z_hot) + dot_nt(v_lo, z_hot)


def incident_kernel(got_ref, comps_ref, weight_ref, column_ref, out_ref, q_hi, q_lo, p_hi, p_lo, f_ref, f_hi, f_lo, t_ref, w_hi, w_lo, v_ref, z_hot):
    blocks = comps_ref.shape[0]
    wide = 2 * HALF * HALF

    f_ref[...] = jnp.zeros_like(f_ref)

    def one_block(i, carry):
        mode_sums(comps_ref[i], weight_ref[...], column_ref[...], q_hi, q_lo, p_hi, p_lo)
        for which in (0, 1):
            f_ref[:, which * wide : (which + 1) * wide] += mode_products(q_hi, q_lo, p_hi, p_lo, which)
        return carry

    lax.fori_loop(0, blocks, one_block, 0)
    f_hi[...], f_lo[...] = split2(f_ref[...])
    x, y, z, cell = slot_rows(got_ref[...])
    point_modes([x, y, z], t_ref)
    chunk = w_hi.shape[1]

    def one_chunk(i, carry):
        point_sums(t_ref, pl.ds(pl.multiple_of(i * chunk, chunk), chunk), f_hi, f_lo, w_hi, w_lo, v_ref)
        return carry

    lax.fori_loop(0, t_ref.shape[2] // chunk, one_chunk, 0)
    depth = out_ref.shape[2]
    place = jnp.floor((cell - 1.0) * (1.0 / depth))
    along = (cell - 1.0) - place * depth
    z_hot[...] = jnp.where(
        along == lax.broadcasted_iota(jnp.int32, z_hot.shape, 0).astype(F32), 1.0, 0.0
    ).astype(BF16)

    def one_field(j, carry):
        out_ref[j] = spread_field(v_ref[pl.ds(j, 1), :], place, z_hot[...], out_ref.shape[1])
        return carry

    lax.fori_loop(0, FIELDS, one_field, 0)


def with_halo(block, sides, width):
    for axis, dim in sides:
        count = lax.axis_size(axis)
        forward = [(i, i + 1) for i in range(count - 1)]
        backward = [(target, source) for source, target in forward]
        low = lax.ppermute(lax.slice_in_dim(block, block.shape[dim] - width, None, axis=dim), axis, forward)
        high = lax.ppermute(lax.slice_in_dim(block, 0, width, axis=dim), axis, backward)
        block = jnp.concatenate([low, block, high], axis=dim)
    return block


def shifted(padded, axis_pos, offset):
    result = padded
    for dim_pos in (1, 2, 3):
        first_cell = 2 + offset if dim_pos == axis_pos else 2
        result = lax.slice_in_dim(result, first_cell, first_cell + padded.shape[dim_pos] - 4, axis=dim_pos)
    return result


def laplace_four(padded):
    summed = centre_weight * shifted(padded, 0, 0)
    for axis_pos in (1, 2, 3):
        summed = summed + near_weight * (shifted(padded, axis_pos, 1) + shifted(padded, axis_pos, -1))
        summed = summed + far_weight * (shifted(padded, axis_pos, 2) + shifted(padded, axis_pos, -2))
    return summed


def local(current_field, earlier_field, wave_coef, layer_mask, point_xyz, point_owner, cell_offset, wave_vector, frequency, amplitude, phase_index, phase_table):
    devices = lax.axis_size("slab") * lax.axis_size("comp")
    points = point_xyz.shape[1]
    width = frequency.shape[0]
    weight, column = mode_tables()
    send, own = pl.pallas_call(
        pack_kernel,
        out_shape=(
            jax.ShapeDtypeStruct((devices, 4 * SLOTS), F32),
            jax.ShapeDtypeStruct((8, width), F32),
        ),
        compiler_params=pltpu.CompilerParams(vmem_limit_bytes=48 << 20),
    )(
        point_owner.reshape(1, points), point_xyz, cell_offset.reshape(1, points), wave_vector,
        frequency.reshape(1, width), amplitude, phase_index.reshape(1, width), phase_table.reshape(-1, 1),
    )
    got = lax.all_to_all(send, ("slab", "comp"), split_axis=0, concat_axis=0, tiled=True)
    comps = lax.all_gather(own, "comp", axis=0)
    _, nx, ny, nz = current_field.shape
    modes = 4 * HALF * HALF
    slots = devices * SLOTS
    chunk = 256
    forcing = pl.pallas_call(
        incident_kernel,
        out_shape=jax.ShapeDtypeStruct((FIELDS, nx * ny, nz), F32),
        scratch_shapes=[
            pltpu.VMEM((2, FIELDS * MODES, width), BF16),
            pltpu.VMEM((2, FIELDS * MODES, width), BF16),
            pltpu.VMEM((2, modes // 2, width), BF16),
            pltpu.VMEM((2, modes // 2, width), BF16),
            pltpu.VMEM((FIELDS * MODES, modes), F32),
            pltpu.VMEM((FIELDS * MODES, modes), BF16),
            pltpu.VMEM((FIELDS * MODES, modes), BF16),
            pltpu.VMEM((3, MODES, slots), F32),
            pltpu.VMEM((modes, chunk), BF16),
            pltpu.VMEM((modes, chunk), BF16),
            pltpu.VMEM((FIELDS, slots), F32),
            pltpu.VMEM((nz, slots), BF16),
        ],
        compiler_params=pltpu.CompilerParams(vmem_limit_bytes=48 << 20),
    )(got, comps, jnp.asarray(weight), jnp.asarray(column))
    forcing = forcing.reshape(FIELDS, nx, ny, nz)
    sign_field = ((layer_mask == 1).astype(F32) - (layer_mask == 2).astype(F32))[None]
    current = current_field
    earlier = earlier_field
    for step_index in range(STEPS):
        widened = with_halo(current, (("slab", 1), ("comp", 2)), 2)
        padded = jnp.pad(widened, ((0, 0), (0, 0), (0, 0), (2, 2)))
        source = forcing[3 * step_index : 3 * step_index + 3]
        following = 2.0 * current - earlier + wave_coef[None] * laplace_four(padded) + sign_field * source
        earlier = current
        current = following
    return (current, earlier)


def solution(mesh):
    in_specs = (
        P(None, "slab", "comp", None),
        P(None, "slab", "comp", None),
        P("slab", "comp", None),
        P("slab", "comp", None),
        P(None, ("slab", "comp")),
        P(("slab", "comp"), None),
        P(("slab", "comp")),
        P(None, "comp"),
        P("comp"),
        P(None, "comp"),
        P("comp"),
        P(),
    )
    out_specs = (P(None, "slab", "comp", None), P(None, "slab", "comp", None))
    return jax.shard_map(local, mesh=mesh, in_specs=in_specs, out_specs=out_specs, check_vma=False)
```

time: 369 us -> 124 us (0.34)
  the two profiles are of different devices: /device:TPU:9 before, /device:TPU:25 now
where the time goes in v1:
time: 124 us; the launch traced here: 123 us
  starting transfers between devices  49.1 us (40%)
  Pallas kernels  27.2 us (22%)
  waiting for transfers between devices  25.1 us (20%)
  local copies, waits for them, and re-layouts  7.77 us (6%)
  blocking collectives  7.22 us (6%)
  other arithmetic  5.84 us (5%)
    pallas_call x1, Pallas kernels, local(): pl.pallas_call(incident_kernel, out_shape=jax.ShapeDtypeStruct((FIELDS, n...  25.4 us
    ppermute x6, starting transfers between devices, with_halo(): lax.ppermute(lax.slice_in_dim(block, 0, width, axis=dim), axis, backward)  23.6 us
    ppermute x6, starting transfers between devices, with_halo(): lax.ppermute(lax.slice_in_dim(block, block.shape[dim] - width, None, axis...  14.9 us
    ppermute x6, waiting for transfers between devices, with_halo(): lax.ppermute(lax.slice_in_dim(block, block.shape[dim] - width, None, axis...  14.4 us
    ppermute x6, waiting for transfers between devices, with_halo(): lax.ppermute(lax.slice_in_dim(block, 0, width, axis=dim), axis, backward)  10.7 us
    all_to_all x1, starting transfers between devices, local(): lax.all_to_all(send, ('slab', 'comp'), split_axis=0, concat_axis=0, tiled...  10.6 us
    all_gather x1, blocking collectives, local(): comps = lax.all_gather(own, 'comp', axis=0)  7.22 us
    unnamed x28, local copies, waits for them, and re-layouts  5.81 us
  transfers between devices with their start and end apart: 13, of which 6 were waited for; matrix products, arithmetic and copies ran while one was open for 2% of the time, Pallas kernels for 21%

profile of v1, /device:TPU:25, one launch (start us, length us, event | category | flops | bytes accessed | tf_op | source)
XLA Modules:
  0.0 123.2 jit_solution(17493501643078530950)
XLA Ops:
  0.6 0.0 copy-start
  0.6 0.8 copy.17.table_ref
  1.5 0.0 copy-start.2
  1.5 0.7 copy-done.2
  2.2 0.0 copy-start.3
  2.2 0.7 copy-done.3
  2.9 0.0 copy-start.4
  2.9 0.7 copy-done.4
  3.6 0.0 copy-start.5
  3.6 0.7 copy-done.5
  4.3 0.7 copy-done.6
  5.0 0.7 copy-done.7
  5.7 0.7 copy-done.8
  6.4 1.7 %shard_map.149 = (f32[128,64]{1,0:T(8,128)}, f32[8,1024]{1,0:T(8,128)S(1)}) custom-call(s32[1,1024]{1,0:T(1,128)S(1)} %bitcast.15, f32[3,1024]{1,0:T(4,128)S(1)} %copy-done.2, s32[1,1024]{1,0:T(1,128)S(1)} %bitcast.16, f32[3,1024]{1,0:T(4,128)S(1)} %copy-done.3, f32[1,1024]{1,0:T(1,128)S(1)} %bitcast.17, f32[3,1024]{1,0:T(4,128)S(1)} %copy-done.4, ...), custom_call_target="tpu_custom_call" | custom-call | tf_op jit(solution)/shard_map/pallas_call | solution.py:254
  8.1 10.6 %all-to-all-start = ((f32[128,1,64]{2,1,0:T(1,128)}), f32[128,1,64]{2,1,0:T(1,128)S(1)}, u32[]{:S(2)}, u32[]{:S(2)}) async-start(f32[128,1,64]{2,1,0:T(1,128)} %bitcast.6), calls=%async_computation | async-start | bytes 131072 | tf_op jit(solution)/shard_map/all_to_all | solution.py:265
  18.7 1.0 fusion.61
  19.7 7.5 %collective-permute-start = (f32[3,2,16,256]{3,2,1,0:T(8,128)S(1)}, f32[3,2,16,256]{3,2,1,0:T(8,128)S(1)}, u32[]{:S(2)}, u32[]{:S(2)}) collective-permute-start(f32[3,2,16,256]{3,2,1,0:T(8,128)S(1)} %get-tuple-element.22), channel_id=1, source_target_pairs={{4,0},{8,4},{12,8},{16,12},{20,16},{24,20},{28,24},{32,28},{36,32}... | collective-permute-start | bytes 294920 | tf_op jit(solution)/shard_map/ppermute | solution.py:228
  27.2 1.9 %collective-permute-start.1 = (f32[3,2,16,256]{3,2,1,0:T(8,128)S(1)}, f32[3,2,16,256]{3,2,1,0:T(8,128)S(1)}, u32[]{:S(2)}, u32[]{:S(2)}) collective-permute-start(f32[3,2,16,256]{3,2,1,0:T(8,128)S(1)} %get-tuple-element.23), channel_id=1, source_target_pairs={{0,4},{4,8},{8,12},{12,16},{16,20},{20,24},{24,28},{28,32},{32,36}... | collective-permute-start | bytes 294920 | tf_op jit(solution)/shard_map/ppermute | solution.py:227
  29.1 0.9 convert_subtract_fusion
  30.1 7.2 %all-gather = f32[32,1024]{1,0:T(8,128)S(1)} all-gather(f32[8,1024]{1,0:T(8,128)S(1)} %get-tuple-element.5), channel_id=2, replica_groups=mesh['slab'=32,'comp'=4] {'comp'}, dimensions={0}, use_global_device_ids=true | all-gather | bytes 163840 | tf_op jit(solution)/shard_map/all_gather | solution.py:266
  37.3 0.0 all-to-all-done
  37.3 0.0 copy-done
  37.3 0.7 copy-done.1
  38.0 25.4 %shard_map.150 = f32[9,128,256]{2,1,0:T(8,128)S(1)} custom-call(f32[128,64]{1,0:T(8,128)S(1)} %bitcast.14, f32[4,8,1024]{2,1,0:T(8,128)S(1)} %bitcast.13, f32[96,96]{1,0:T(8,128)S(1)} %copy-done, f32[48,128]{1,0:T(8,128)S(1)} %copy-done.1), custom_call_target="tpu_custom_call" | custom-call | tf_op jit(solution)/shard_map/pallas_call | solution.py:271
  63.5 0.0 collective-permute-done.1
  63.5 0.0 copy-done.10
  63.5 0.1 constant_dynamic-update-slice_fusion.1
  63.7 0.0 collective-permute-done
  63.7 0.1 fusion.58
  63.8 2.0 %collective-permute-start.3 = (f32[3,12,2,256]{3,2,1,0:T(2,128)S(1)}, f32[3,12,2,256]{3,2,1,0:T(2,128)S(1)}, u32[]{:S(2)}, u32[]{:S(2)}) collective-permute-start(f32[3,12,2,256]{3,2,1,0:T(2,128)S(1)} %get-tuple-element.13), channel_id=1, source_target_pairs={{0,1},{1,2},{2,3},{4,5},{5,6},{6,7},{8,9},{9,10},{10,11},{12,13},{... | collective-permute-start | bytes 221192 | tf_op jit(solution)/shard_map/ppermute | solution.py:227
  65.8 2.3 %collective-permute-start.2 = (f32[3,12,2,256]{3,2,1,0:T(2,128)S(1)}, f32[3,12,2,256]{3,2,1,0:T(2,128)S(1)}, u32[]{:S(2)}, u32[]{:S(2)}) collective-permute-start(f32[3,12,2,256]{3,2,1,0:T(2,128)S(1)} %get-tuple-element.14), channel_id=1, source_target_pairs={{1,0},{2,1},{3,2},{5,4},{6,5},{7,6},{9,8},{10,9},{11,10},{13,12},{... | collective-permute-start | bytes 221192 | tf_op jit(solution)/shard_map/ppermute | solution.py:228
  68.1 0.1 fusion.57
  68.2 0.0 copy-start.11
  68.2 0.0 copy-start.12
  68.2 0.0 collective-permute-done.3
  68.2 3.2 %collective-permute-done.2 = f32[3,12,2,256]{3,2,1,0:T(2,128)S(1)} collective-permute-done((f32[3,12,2,256]{3,2,1,0:T(2,128)S(1)}, f32[3,12,2,256]{3,2,1,0:T(2,128)S(1)}, u32[]{:S(2)}, u32[]{:S(2)}) %collective-permute-start.2) | collective-permute-done | bytes 73760 | tf_op jit(solution)/shard_map/ppermute | solution.py:228
  71.4 0.7 select_maximum_fusion.8
  72.1 0.0 copy-done.11
  72.1 0.0 copy-done.12
  72.2 0.6 fusion.45
  72.8 8.0 %collective-permute-start.4 = (f32[3,2,16,256]{3,2,1,0:T(8,128)S(1)}, f32[3,2,16,256]{3,2,1,0:T(8,128)S(1)}, u32[]{:S(2)}, u32[]{:S(2)}) collective-permute-start(f32[3,2,16,256]{3,2,1,0:T(8,128)S(1)} %get-tuple-element.17), channel_id=1, source_target_pairs={{4,0},{8,4},{12,8},{16,12},{20,16},{24,20},{28,24},{32,28},{36,32}... | collective-permute-start | bytes 294920 | tf_op jit(solution)/shard_map/ppermute | solution.py:228
  80.8 1.9 %collective-permute-start.5 = (f32[3,2,16,256]{3,2,1,0:T(8,128)S(1)}, f32[3,2,16,256]{3,2,1,0:T(8,128)S(1)}, u32[]{:S(2)}, u32[]{:S(2)}) collective-permute-start(f32[3,2,16,256]{3,2,1,0:T(8,128)S(1)} %get-tuple-element.18), channel_id=1, source_target_pairs={{0,4},{4,8},{8,12},{12,16},{16,20},{20,24},{24,28},{28,32},{32,36}... | collective-permute-start | bytes 294920 | tf_op jit(solution)/shard_map/ppermute | solution.py:227
  82.7 0.0 collective-permute-done.4
  82.7 7.9 %collective-permute-done.5 = f32[3,2,16,256]{3,2,1,0:T(8,128)S(1)} collective-permute-done((f32[3,2,16,256]{3,2,1,0:T(8,128)S(1)}, f32[3,2,16,256]{3,2,1,0:T(8,128)S(1)}, u32[]{:S(2)}, u32[]{:S(2)}) %collective-permute-start.5) | collective-permute-done | bytes 98336 | tf_op jit(solution)/shard_map/ppermute | solution.py:227
  90.7 0.1 pad_maximum_fusion.21
  90.7 2.7 %collective-permute-start.7 = (f32[3,12,2,256]{3,2,1,0:T(2,128)S(1)}, f32[3,12,2,256]{3,2,1,0:T(2,128)S(1)}, u32[]{:S(2)}, u32[]{:S(2)}) collective-permute-start(f32[3,12,2,256]{3,2,1,0:T(2,128)S(1)} %get-tuple-element.11), channel_id=1, source_target_pairs={{0,1},{1,2},{2,3},{4,5},{5,6},{6,7},{8,9},{9,10},{10,11},{12,13},{... | collective-permute-start | bytes 221192 | tf_op jit(solution)/shard_map/ppermute | solution.py:227
  93.4 1.9 %collective-permute-start.6 = (f32[3,12,2,256]{3,2,1,0:T(2,128)S(1)}, f32[3,12,2,256]{3,2,1,0:T(2,128)S(1)}, u32[]{:S(2)}, u32[]{:S(2)}) collective-permute-start(f32[3,12,2,256]{3,2,1,0:T(2,128)S(1)} %get-tuple-element.12), channel_id=1, source_target_pairs={{1,0},{2,1},{3,2},{5,4},{6,5},{7,6},{9,8},{10,9},{11,10},{13,12},{... | collective-permute-start | bytes 221192 | tf_op jit(solution)/shard_map/ppermute | solution.py:228
  95.4 0.0 collective-permute-done.7
  95.4 3.7 %collective-permute-done.6 = f32[3,12,2,256]{3,2,1,0:T(2,128)S(1)} collective-permute-done((f32[3,12,2,256]{3,2,1,0:T(2,128)S(1)}, f32[3,12,2,256]{3,2,1,0:T(2,128)S(1)}, u32[]{:S(2)}, u32[]{:S(2)}) %collective-permute-start.6) | collective-permute-done | bytes 73760 | tf_op jit(solution)/shard_map/ppermute | solution.py:228
  99.1 0.7 select_maximum_fusion.4
  99.8 0.7 fusion.25
  100.5 0.0 copy-start.9
  100.5 1.9 %collective-permute-start.8 = (f32[3,2,16,256]{3,2,1,0:T(8,128)S(1)}, f32[3,2,16,256]{3,2,1,0:T(8,128)S(1)}, u32[]{:S(2)}, u32[]{:S(2)}) collective-permute-start(f32[3,2,16,256]{3,2,1,0:T(8,128)S(1)} %get-tuple-element.15), channel_id=1, source_target_pairs={{4,0},{8,4},{12,8},{16,12},{20,16},{24,20},{28,24},{32,28},{36,32}... | collective-permute-start | bytes 294920 | tf_op jit(solution)/shard_map/ppermute | solution.py:228
  102.4 3.4 %collective-permute-start.9 = (f32[3,2,16,256]{3,2,1,0:T(8,128)S(1)}, f32[3,2,16,256]{3,2,1,0:T(8,128)S(1)}, u32[]{:S(2)}, u32[]{:S(2)}) collective-permute-start(f32[3,2,16,256]{3,2,1,0:T(8,128)S(1)} %get-tuple-element.16), channel_id=1, source_target_pairs={{0,4},{4,8},{8,12},{12,16},{16,20},{20,24},{24,28},{28,32},{32,36}... | collective-permute-start | bytes 294920 | tf_op jit(solution)/shard_map/ppermute | solution.py:227
  105.8 0.1 collective-permute-done.8
  105.9 6.4 %collective-permute-done.9 = f32[3,2,16,256]{3,2,1,0:T(8,128)S(1)} collective-permute-done((f32[3,2,16,256]{3,2,1,0:T(8,128)S(1)}, f32[3,2,16,256]{3,2,1,0:T(8,128)S(1)}, u32[]{:S(2)}, u32[]{:S(2)}) %collective-permute-start.9) | collective-permute-done | bytes 98336 | tf_op jit(solution)/shard_map/ppermute | solution.py:227
  112.3 0.1 pad_maximum_fusion.18
  112.4 3.0 %collective-permute-start.11 = (f32[3,12,2,256]{3,2,1,0:T(2,128)S(1)}, f32[3,12,2,256]{3,2,1,0:T(2,128)S(1)}, u32[]{:S(2)}, u32[]{:S(2)}) collective-permute-start(f32[3,12,2,256]{3,2,1,0:T(2,128)S(1)} %get-tuple-element.9), channel_id=1, source_target_pairs={{0,1},{1,2},{2,3},{4,5},{5,6},{6,7},{8,9},{9,10},{10,11},{12,13},{... | collective-permute-start | bytes 221192 | tf_op jit(solution)/shard_map/ppermute | solution.py:227
  115.4 1.9 %collective-permute-start.10 = (f32[3,12,2,256]{3,2,1,0:T(2,128)S(1)}, f32[3,12,2,256]{3,2,1,0:T(2,128)S(1)}, u32[]{:S(2)}, u32[]{:S(2)}) collective-permute-start(f32[3,12,2,256]{3,2,1,0:T(2,128)S(1)} %get-tuple-element.10), channel_id=1, source_target_pairs={{1,0},{2,1},{3,2},{5,4},{6,5},{7,6},{9,8},{10,9},{11,10},{13,12},{... | collective-permute-start | bytes 221192 | tf_op jit(solution)/shard_map/ppermute | solution.py:228
  117.3 0.0 collective-permute-done.11
  117.3 3.7 %collective-permute-done.10 = f32[3,12,2,256]{3,2,1,0:T(2,128)S(1)} collective-permute-done((f32[3,12,2,256]{3,2,1,0:T(2,128)S(1)}, f32[3,12,2,256]{3,2,1,0:T(2,128)S(1)}, u32[]{:S(2)}, u32[]{:S(2)}) %collective-permute-start.10) | collective-permute-done | bytes 73760 | tf_op jit(solution)/shard_map/ppermute | solution.py:228
  121.1 0.7 select_maximum_fusion
  121.8 0.0 copy-done.9
  121.8 1.4 %fusion.12 = f32[3,8,16,256]{3,2,1,0:T(8,128)} fusion(f32[3,2,16,256]{3,2,1,0:T(8,128)S(1)} %collective-permute-done.9, f32[3,8,16,256]{3,2,1,0:T(8,128)S(1)} %fusion.25, f32[3,2,16,256]{3,2,1,0:T(8,128)S(1)} %collective-permute-done.8, f32[3,12,20,260]{3,2,1,0:T(8,128)S(1)} %select_maximum_fusion, f32[3,12,2,256]{3,2,1,0:T(2,128)S(1)} %collective-permute-done.11, ...), kind=kLoop, calls=%fused_computation.32 | loop fusion | flops 4030464 | bytes 3751936 | tf_op jit(solution)/shard_map/add | solution.py:298
  (9 shorter events, 0.1 us)
Async XLA Ops:
  0.6 36.7 %copy-start = (f32[96,96]{1,0:T(8,128)S(1)}, f32[96,96]{1,0:T(8,128)}, u32[]{:S(2)}) copy-start(f32[96,96]{1,0:T(8,128)} %constant.19.clone.weight_ref) | copy-start | bytes 110596
  1.5 0.7 copy-start.2
  2.2 0.7 copy-start.3
  2.9 0.7 copy-start.4
  3.6 0.7 copy-start.5
  4.3 0.7 copy-start.6
  5.0 0.7 copy-start.7
  5.7 0.7 copy-start.8
  8.1 55.4 %copy-start.10 = (f32[3,8,16,256]{3,2,1,0:T(8,128)S(1)}, f32[3,8,16,256]{3,2,1,0:T(8,128)}, u32[]{:S(2)}) copy-start(f32[3,8,16,256]{3,2,1,0:T(8,128)} %param.14) | copy-start | bytes 1179652
  8.1 29.2 %all-to-all-start = ((f32[128,1,64]{2,1,0:T(1,128)}), f32[128,1,64]{2,1,0:T(1,128)S(1)}, u32[]{:S(2)}, u32[]{:S(2)}) async-start(f32[128,1,64]{2,1,0:T(1,128)} %bitcast.6), calls=%async_computation | async-start | bytes 131072 | tf_op jit(solution)/shard_map/all_to_all | solution.py:265
  19.7 44.0 %collective-permute-start = (f32[3,2,16,256]{3,2,1,0:T(8,128)S(1)}, f32[3,2,16,256]{3,2,1,0:T(8,128)S(1)}, u32[]{:S(2)}, u32[]{:S(2)}) collective-permute-start(f32[3,2,16,256]{3,2,1,0:T(8,128)S(1)} %get-tuple-element.22), channel_id=1, source_target_pairs={{4,0},{8,4},{12,8},{16,12},{20,16},{24,20},{28,24},{32,28},{36,32}... | collective-permute-start | bytes 294920 | tf_op jit(solution)/shard_map/ppermute | solution.py:228
  27.2 36.3 %collective-permute-start.1 = (f32[3,2,16,256]{3,2,1,0:T(8,128)S(1)}, f32[3,2,16,256]{3,2,1,0:T(8,128)S(1)}, u32[]{:S(2)}, u32[]{:S(2)}) collective-permute-start(f32[3,2,16,256]{3,2,1,0:T(8,128)S(1)} %get-tuple-element.23), channel_id=1, source_target_pairs={{0,4},{4,8},{8,12},{12,16},{16,20},{20,24},{24,28},{28,32},{32,36}... | collective-permute-start | bytes 294920 | tf_op jit(solution)/shard_map/ppermute | solution.py:227
  37.3 0.7 copy-start.1
  63.8 4.5 %collective-permute-start.3 = (f32[3,12,2,256]{3,2,1,0:T(2,128)S(1)}, f32[3,12,2,256]{3,2,1,0:T(2,128)S(1)}, u32[]{:S(2)}, u32[]{:S(2)}) collective-permute-start(f32[3,12,2,256]{3,2,1,0:T(2,128)S(1)} %get-tuple-element.13), channel_id=1, source_target_pairs={{0,1},{1,2},{2,3},{4,5},{5,6},{6,7},{8,9},{9,10},{10,11},{12,13},{... | collective-permute-start | bytes 221192 | tf_op jit(solution)/shard_map/ppermute | solution.py:227
  65.8 5.7 %collective-permute-start.2 = (f32[3,12,2,256]{3,2,1,0:T(2,128)S(1)}, f32[3,12,2,256]{3,2,1,0:T(2,128)S(1)}, u32[]{:S(2)}, u32[]{:S(2)}) collective-permute-start(f32[3,12,2,256]{3,2,1,0:T(2,128)S(1)} %get-tuple-element.14), channel_id=1, source_target_pairs={{1,0},{2,1},{3,2},{5,4},{6,5},{7,6},{9,8},{10,9},{11,10},{13,12},{... | collective-permute-start | bytes 221192 | tf_op jit(solution)/shard_map/ppermute | solution.py:228
  68.2 3.9 %copy-start.11 = (f32[8,16,256]{2,1,0:T(8,128)S(1)}, f32[8,16,256]{2,1,0:T(8,128)}, u32[]{:S(2)}) copy-start(f32[8,16,256]{2,1,0:T(8,128)} %param.16) | copy-start | bytes 393220
  68.2 3.9 %copy-start.12 = (f32[3,8,16,256]{3,2,1,0:T(8,128)S(1)}, f32[3,8,16,256]{3,2,1,0:T(8,128)}, u32[]{:S(2)}) copy-start(f32[3,8,16,256]{3,2,1,0:T(8,128)} %param.15) | copy-start | bytes 1179652
  72.8 9.9 %collective-permute-start.4 = (f32[3,2,16,256]{3,2,1,0:T(8,128)S(1)}, f32[3,2,16,256]{3,2,1,0:T(8,128)S(1)}, u32[]{:S(2)}, u32[]{:S(2)}) collective-permute-start(f32[3,2,16,256]{3,2,1,0:T(8,128)S(1)} %get-tuple-element.17), channel_id=1, source_target_pairs={{4,0},{8,4},{12,8},{16,12},{20,16},{24,20},{28,24},{32,28},{36,32}... | collective-permute-start | bytes 294920 | tf_op jit(solution)/shard_map/ppermute | solution.py:228
  80.8 9.9 %collective-permute-start.5 = (f32[3,2,16,256]{3,2,1,0:T(8,128)S(1)}, f32[3,2,16,256]{3,2,1,0:T(8,128)S(1)}, u32[]{:S(2)}, u32[]{:S(2)}) collective-permute-start(f32[3,2,16,256]{3,2,1,0:T(8,128)S(1)} %get-tuple-element.18), channel_id=1, source_target_pairs={{0,4},{4,8},{8,12},{12,16},{16,20},{20,24},{24,28},{28,32},{32,36}... | collective-permute-start | bytes 294920 | tf_op jit(solution)/shard_map/ppermute | solution.py:227
  90.7 4.6 %collective-permute-start.7 = (f32[3,12,2,256]{3,2,1,0:T(2,128)S(1)}, f32[3,12,2,256]{3,2,1,0:T(2,128)S(1)}, u32[]{:S(2)}, u32[]{:S(2)}) collective-permute-start(f32[3,12,2,256]{3,2,1,0:T(2,128)S(1)} %get-tuple-element.11), channel_id=1, source_target_pairs={{0,1},{1,2},{2,3},{4,5},{5,6},{6,7},{8,9},{9,10},{10,11},{12,13},{... | collective-permute-start | bytes 221192 | tf_op jit(solution)/shard_map/ppermute | solution.py:227
  93.4 5.7 %collective-permute-start.6 = (f32[3,12,2,256]{3,2,1,0:T(2,128)S(1)}, f32[3,12,2,256]{3,2,1,0:T(2,128)S(1)}, u32[]{:S(2)}, u32[]{:S(2)}) collective-permute-start(f32[3,12,2,256]{3,2,1,0:T(2,128)S(1)} %get-tuple-element.12), channel_id=1, source_target_pairs={{1,0},{2,1},{3,2},{5,4},{6,5},{7,6},{9,8},{10,9},{11,10},{13,12},{... | collective-permute-start | bytes 221192 | tf_op jit(solution)/shard_map/ppermute | solution.py:228
  100.5 21.3 %copy-start.9 = (f32[3,8,16,256]{3,2,1,0:T(8,128)}, f32[3,8,16,256]{3,2,1,0:T(8,128)S(1)}, u32[]{:S(2)}) copy-start(f32[3,8,16,256]{3,2,1,0:T(8,128)S(1)} %fusion.25) | copy-start | bytes 1179652
  100.5 5.4 %collective-permute-start.8 = (f32[3,2,16,256]{3,2,1,0:T(8,128)S(1)}, f32[3,2,16,256]{3,2,1,0:T(8,128)S(1)}, u32[]{:S(2)}, u32[]{:S(2)}) collective-permute-start(f32[3,2,16,256]{3,2,1,0:T(8,128)S(1)} %get-tuple-element.15), channel_id=1, source_target_pairs={{4,0},{8,4},{12,8},{16,12},{20,16},{24,20},{28,24},{32,28},{36,32}... | collective-permute-start | bytes 294920 | tf_op jit(solution)/shard_map/ppermute | solution.py:228
  102.4 9.9 %collective-permute-start.9 = (f32[3,2,16,256]{3,2,1,0:T(8,128)S(1)}, f32[3,2,16,256]{3,2,1,0:T(8,128)S(1)}, u32[]{:S(2)}, u32[]{:S(2)}) collective-permute-start(f32[3,2,16,256]{3,2,1,0:T(8,128)S(1)} %get-tuple-element.16), channel_id=1, source_target_pairs={{0,4},{4,8},{8,12},{12,16},{16,20},{20,24},{24,28},{28,32},{32,36}... | collective-permute-start | bytes 294920 | tf_op jit(solution)/shard_map/ppermute | solution.py:227
  112.4 4.9 %collective-permute-start.11 = (f32[3,12,2,256]{3,2,1,0:T(2,128)S(1)}, f32[3,12,2,256]{3,2,1,0:T(2,128)S(1)}, u32[]{:S(2)}, u32[]{:S(2)}) collective-permute-start(f32[3,12,2,256]{3,2,1,0:T(2,128)S(1)} %get-tuple-element.9), channel_id=1, source_target_pairs={{0,1},{1,2},{2,3},{4,5},{5,6},{6,7},{8,9},{9,10},{10,11},{12,13},{... | collective-permute-start | bytes 221192 | tf_op jit(solution)/shard_map/ppermute | solution.py:227
  115.4 5.7 %collective-permute-start.10 = (f32[3,12,2,256]{3,2,1,0:T(2,128)S(1)}, f32[3,12,2,256]{3,2,1,0:T(2,128)S(1)}, u32[]{:S(2)}, u32[]{:S(2)}) collective-permute-start(f32[3,12,2,256]{3,2,1,0:T(2,128)S(1)} %get-tuple-element.10), channel_id=1, source_target_pairs={{1,0},{2,1},{3,2},{5,4},{6,5},{7,6},{9,8},{10,9},{11,10},{13,12},{... | collective-permute-start | bytes 221192 | tf_op jit(solution)/shard_map/ppermute | solution.py:228

commit v2 on v1

--- a/solution.py
+++ b/solution.py
@@ -15,6 +15,7 @@
 FIELDS = 9
 F32 = jnp.float32
 BF16 = jnp.bfloat16
+MESH = pl.DeviceIdType.MESH
 
 step_size = 0.05
 near_weight = 4.0 / 3.0
@@ -77,34 +78,6 @@
 
 def dot_nn(a, b):
     return lax.dot_general(a, b, (((1,), (0,)), ((), ())), preferred_element_type=F32)
-
-
-def pack_kernel(owner_ref, xyz_ref, offset_ref, wave_ref, freq_ref, amp_ref, index_ref, table_ref, send_ref, comp_ref):
-    points = owner_ref.shape[1]
-    devices = send_ref.shape[0]
-    hit = owner_ref[...] == lax.broadcasted_iota(jnp.int32, (devices, points), 0)
-    match = jnp.where(hit, 1.0, 0.0)
-    match16 = match.astype(BF16)
-    before = (
-        lax.broadcasted_iota(jnp.int32, (points, points), 0)
-        < lax.broadcasted_iota(jnp.int32, (points, points), 1)
-    )
-    count = dot_nn(match16, jnp.where(before, 1.0, 0.0).astype(BF16))
-    rank = jnp.sum(count * match, axis=0, keepdims=True)
-    slot = rank == lax.broadcasted_iota(jnp.int32, (SLOTS, points), 0).astype(F32)
-    values = [xyz_ref[i : i + 1, :] for i in range(3)] + [(offset_ref[...] + 1).astype(F32)]
-    spread = jnp.concatenate([jnp.where(slot, v, 0.0) for v in values], axis=0)
-    first, rest = split2(spread)
-    rest = spread - first.astype(F32)
-    second, third = split2(rest)
-    send_ref[...] = dot_nt(match16, first) + dot_nt(match16, second) + dot_nt(match16, third)
-    entries = table_ref.shape[0]
-    found = index_ref[...] == lax.broadcasted_iota(jnp.int32, (entries, index_ref.shape[1]), 0)
-    phase = jnp.sum(jnp.where(found, table_ref[...], 0.0), axis=0, keepdims=True)
-    comp_ref[0:3, :] = wave_ref[...]
-    comp_ref[3:4, :] = freq_ref[...]
-    comp_ref[4:7, :] = amp_ref[...]
-    comp_ref[7:8, :] = phase
 
 
 def mode_sums(block, weight, column, q_hi, q_lo, p_hi, p_lo):
@@ -182,22 +155,225 @@
     return dot_nt(v_hi, z_hot) + dot_nt(v_lo, z_hot)
 
 
-def incident_kernel(got_ref, comps_ref, weight_ref, column_ref, out_ref, q_hi, q_lo, p_hi, p_lo, f_ref, f_hi, f_lo, t_ref, w_hi, w_lo, v_ref, z_hot):
-    blocks = comps_ref.shape[0]
+def pack_points(owner, xyz, offset, send, split):
+    in_row, in_column, in_group = split
+    points = owner.shape[1]
+    devices = in_row * in_column * in_group
+    c = owner & (in_group - 1)
+    slab = owner >> (in_group.bit_length() - 1)
+    w, y = slab & (in_row - 1), slab >> (in_row.bit_length() - 1)
+    place = (w * in_column + y) * in_group + c
+    hit = place == lax.broadcasted_iota(jnp.int32, (devices, points), 0)
+    match = jnp.where(hit, 1.0, 0.0)
+    match16 = match.astype(BF16)
+    before = (
+        lax.broadcasted_iota(jnp.int32, (points, points), 0)
+        < lax.broadcasted_iota(jnp.int32, (points, points), 1)
+    )
+    count = dot_nn(match16, jnp.where(before, 1.0, 0.0).astype(BF16))
+    rank = jnp.sum(count * match, axis=0, keepdims=True)
+    slot = rank == lax.broadcasted_iota(jnp.int32, (SLOTS, points), 0).astype(F32)
+    values = [xyz[i : i + 1, :] for i in range(3)] + [(offset + 1).astype(F32)]
+    spread = jnp.concatenate([jnp.where(slot, v, 0.0) for v in values], axis=0)
+    first = spread.astype(BF16)
+    second, third = split2(spread - first.astype(F32))
+    rows = dot_nt(match16, first) + dot_nt(match16, second) + dot_nt(match16, third)
+    for d in range(devices):
+        send[d // (in_column * in_group), d // in_group % in_column, d % in_group] = rows[d : d + 1, :]
+
+
+def wave_kernel(
+    split,
+    current_in, earlier_in, coef_in, mask_in, owner_in, xyz_in, offset_in, wave_in, freq_in, amp_in, index_in, table_in,
+    weight_in, column_in,
+    final_ref, prior_ref,
+    held, driven, coef, mask, sign, owner, xyz, offset, wave, freq, amp, index, table, weight, column, load_sem,
+    comps, comp_send, comp_recv,
+    sent, first, second, third, hop_send, hop_recv, hop_own,
+    x_in, y_in, y_out, halo_send, halo_recv,
+    q_hi, q_lo, p_hi, p_lo, f_ref, f_hi, f_lo, t_ref, w_hi, w_lo, v_ref, z_hot, forcing,
+):
+    in_row, in_column, in_group = split
+    slabs = in_row * in_column
+    slab, comp = lax.axis_index("slab"), lax.axis_index("comp")
+    y, w = slab // in_row, slab % in_row
+    nx, ny, nz = coef.shape
+    after, before = lax.rem(slab + 1, slabs), lax.rem(slab + slabs - 1, slabs)
+    right, left = lax.rem(comp + 1, in_group), lax.rem(comp + in_group - 1, in_group)
+
+    def row_at(d):
+        return lax.rem(w + d, in_row)
+
+    def column_at(d):
+        return lax.rem(y + d, in_column)
+
+    def group_at(d):
+        return lax.rem(comp + d, in_group)
+
+    barrier = pltpu.get_barrier_semaphore()
+    partners = [(y * in_row + row_at(d), comp) for d in range(1, in_row)]
+    partners += [(column_at(d) * in_row + w, comp) for d in range(1, in_column)]
+    partners += [(slab, group_at(d)) for d in range(1, in_group)]
+    partners += [(after, comp), (before, comp)]
+    for partner in partners:
+        pl.semaphore_signal(barrier, inc=1, device_id=partner, device_id_type=MESH)
+
+    loads = [
+        pltpu.make_async_copy(a, b, load_sem.at[i])
+        for i, (a, b) in enumerate((
+            (owner_in, owner), (xyz_in, xyz), (offset_in, offset),
+            (wave_in, wave), (freq_in, freq), (amp_in, amp), (index_in, index), (table_in, table),
+            (current_in, held.at[1]), (column_in, column), (weight_in, weight),
+            (coef_in, coef), (earlier_in, held.at[0]), (mask_in, mask),
+        ))
+    ]
+    for load in loads:
+        load.start()
+    for load in loads[:3]:
+        load.wait()
+    pack_points(owner[...], xyz[...], offset[...], sent, split)
+    for load in loads[3:8]:
+        load.wait()
+    found = index[...] == lax.broadcasted_iota(jnp.int32, (table.shape[1], index.shape[1]), 0)
+    phase = lax.dot_general(
+        table[...], jnp.where(found, 1.0, 0.0), (((1,), (0,)), ((), ())),
+        precision=lax.Precision.HIGHEST, preferred_element_type=F32,
+    )
+    comps[0, 0:3, :] = wave[...]
+    comps[0, 3:4, :] = freq[...]
+    comps[0, 4:7, :] = amp[...]
+    comps[0, 7:8, :] = phase
+    loads[8].wait()
+
+    def halo_copies(e, u):
+        faces = (
+            (u.at[:, pl.ds(0, 2)], x_in.at[e, 1], (before, comp)),
+            (u.at[:, pl.ds(nx - 2, 2)], x_in.at[e, 0], (after, comp)),
+            (y_out.at[e, 0], y_in.at[e, 1], (slab, left)),
+            (y_out.at[e, 1], y_in.at[e, 0], (slab, right)),
+        )
+        return [
+            pltpu.make_async_remote_copy(
+                src_ref=a, dst_ref=b, send_sem=halo_send.at[e, i], recv_sem=halo_recv.at[e, i],
+                device_id=target, device_id_type=MESH,
+            )
+            for i, (a, b, target) in enumerate(faces)
+        ]
+
+    def start_halo(e, u):
+        y_out[e, 0] = u[:, :, 0:2, :]
+        y_out[e, 1] = u[:, :, ny - 2 : ny, :]
+        for copy in halo_copies(e, u):
+            copy.start()
+
+    def wait_halo(e, u):
+        for copy in halo_copies(e, u):
+            copy.wait()
+
+    def comp_copy(d):
+        return pltpu.make_async_remote_copy(
+            src_ref=comps.at[0], dst_ref=comps.at[d], send_sem=comp_send.at[d], recv_sem=comp_recv.at[d],
+            device_id=(slab, group_at(d)), device_id_type=MESH,
+        )
+
+    def hop_copies(hop):
+        if hop == 0:
+            moves = [(sent.at[row_at(d)], first.at[w], (y * in_row + row_at(d), comp)) for d in range(in_row)]
+        elif hop == 1:
+            moves = [
+                (first.at[:, column_at(d)], second.at[y], (column_at(d) * in_row + w, comp)) for d in range(in_column)
+            ]
+        else:
+            moves = [(second.at[:, :, group_at(d)], third.at[comp], (slab, group_at(d))) for d in range(in_group)]
+        own = pltpu.make_async_copy(moves[0][0], moves[0][1], hop_own.at[hop])
+        return [own] + [
+            pltpu.make_async_remote_copy(
+                src_ref=a, dst_ref=b, send_sem=hop_send.at[hop, d], recv_sem=hop_recv.at[hop, d],
+                device_id=target, device_id_type=MESH,
+            )
+            for d, (a, b, target) in enumerate(moves) if d > 0
+        ]
+
+    def start_hop(hop):
+        for copy in hop_copies(hop):
+            copy.start()
+
+    def wait_hop(hop):
+        for copy in hop_copies(hop):
+            copy.wait()
+
+    pl.semaphore_wait(barrier, len(partners))
+    for d in range(1, in_group):
+        comp_copy(d).start()
+    start_hop(0)
+    start_halo(0, held.at[1])
+    for load in loads[9:]:
+        load.wait()
+    sign[...] = jnp.where(mask[...] == 1, 1.0, 0.0) - jnp.where(mask[...] == 2, 1.0, 0.0)
+
+    lane = lax.broadcasted_iota(jnp.int32, (ny, nz), 1)
+
+    def advance(e, field, i, source):
+        def one(c, carry):
+            low, high = x_in[e, 0, c], x_in[e, 1, c]
+            low, high = jnp.where(slab > 0, low, 0.0), jnp.where(slab < slabs - 1, high, 0.0)
+            planes = [low[0], low[1]] + [field[i + 1, c, x] for x in range(nx)] + [high[0], high[1]]
+            for x in range(nx):
+                u = planes[x + 2]
+                back = jnp.where(comp > 0, y_in[e, 0, c, x], 0.0)
+                front = jnp.where(comp < in_group - 1, y_in[e, 1, c, x], 0.0)
+                tall = jnp.concatenate([back, u, front], axis=0)
+                near = planes[x + 1] + planes[x + 3]
+                far = planes[x] + planes[x + 4]
+                near = near + (tall[1 : ny + 1] + tall[3 : ny + 3])
+                far = far + (tall[0:ny] + tall[4 : ny + 4])
+                near = near + jnp.where(lane >= 1, pltpu.roll(u, 1, 1), 0.0)
+                near = near + jnp.where(lane < nz - 1, pltpu.roll(u, nz - 1, 1), 0.0)
+                far = far + jnp.where(lane >= 2, pltpu.roll(u, 2, 1), 0.0)
+                far = far + jnp.where(lane < nz - 2, pltpu.roll(u, nz - 2, 1), 0.0)
+                curved = centre_weight * u + near_weight * near + far_weight * far
+                following = 2.0 * u - field[i, c, x] + coef[x] * curved
+                if source is not None:
+                    following = following + source(c, x)
+                field[i + 2, c, x] = following
+            return carry
+
+        lax.fori_loop(0, 3, one, 0)
+
     wide = 2 * HALF * HALF
-
     f_ref[...] = jnp.zeros_like(f_ref)
 
     def one_block(i, carry):
-        mode_sums(comps_ref[i], weight_ref[...], column_ref[...], q_hi, q_lo, p_hi, p_lo)
+        @pl.when(i > 0)
+        def _():
+            comp_copy(i).wait()
+
+        mode_sums(comps[i], weight[...], column[...], q_hi, q_lo, p_hi, p_lo)
         for which in (0, 1):
             f_ref[:, which * wide : (which + 1) * wide] += mode_products(q_hi, q_lo, p_hi, p_lo, which)
+
+        for hop in (0, 1):
+            @pl.when(i == hop)
+            def _(hop=hop):
+                wait_hop(hop)
+                start_hop(hop + 1)
+
+        @pl.when(i < STEPS)
+        def _():
+            wait_halo(i, held.at[i + 1])
+            advance(i, held, i, None)
+
+            @pl.when(i < STEPS - 1)
+            def _():
+                start_halo(i + 1, held.at[i + 2])
+
         return carry
 
-    lax.fori_loop(0, blocks, one_block, 0)
+    lax.fori_loop(0, in_group, one_block, 0)
     f_hi[...], f_lo[...] = split2(f_ref[...])
-    x, y, z, cell = slot_rows(got_ref[...])
-    point_modes([x, y, z], t_ref)
+    wait_hop(2)
+    px, py, pz, cell = slot_rows(third[...].reshape(in_group * slabs, 4 * SLOTS))
+    point_modes([px, py, pz], t_ref)
     chunk = w_hi.shape[1]
 
     def one_chunk(i, carry):
@@ -205,73 +381,89 @@
         return carry
 
     lax.fori_loop(0, t_ref.shape[2] // chunk, one_chunk, 0)
-    depth = out_ref.shape[2]
-    place = jnp.floor((cell - 1.0) * (1.0 / depth))
-    along = (cell - 1.0) - place * depth
+    place = jnp.floor((cell - 1.0) * (1.0 / nz))
+    along = (cell - 1.0) - place * nz
     z_hot[...] = jnp.where(
         along == lax.broadcasted_iota(jnp.int32, z_hot.shape, 0).astype(F32), 1.0, 0.0
     ).astype(BF16)
-
-    def one_field(j, carry):
-        out_ref[j] = spread_field(v_ref[pl.ds(j, 1), :], place, z_hot[...], out_ref.shape[1])
+    driven[0] = jnp.zeros_like(driven[0])
+
+    def one_step(n, carry):
+        def one_field(i, inner):
+            j = 3 * n + i
+            forcing[i] = spread_field(v_ref[pl.ds(j, 1), :], place, z_hot[...], nx * ny)
+            return inner
+
+        lax.fori_loop(0, 3, one_field, 0)
+
+        def source(c, x):
+            return sign[x] * forcing[c, x * ny : (x + 1) * ny, :]
+
+        @pl.when(n == 0)
+        def _():
+            def one(c, inner):
+                for x in range(nx):
+                    driven[1, c, x] = source(c, x)
+                return inner
+
+            lax.fori_loop(0, 3, one, 0)
+
+        @pl.when(n > 0)
+        def _():
+            wait_halo(STEPS + n - 1, driven.at[n])
+            advance(STEPS + n - 1, driven, n - 1, source)
+
+        @pl.when(n < STEPS - 1)
+        def _():
+            start_halo(STEPS + n, driven.at[n + 1])
+
         return carry
 
-    lax.fori_loop(0, FIELDS, one_field, 0)
-
-
-def with_halo(block, sides, width):
-    for axis, dim in sides:
-        count = lax.axis_size(axis)
-        forward = [(i, i + 1) for i in range(count - 1)]
-        backward = [(target, source) for source, target in forward]
-        low = lax.ppermute(lax.slice_in_dim(block, block.shape[dim] - width, None, axis=dim), axis, forward)
-        high = lax.ppermute(lax.slice_in_dim(block, 0, width, axis=dim), axis, backward)
-        block = jnp.concatenate([low, block, high], axis=dim)
-    return block
-
-
-def shifted(padded, axis_pos, offset):
-    result = padded
-    for dim_pos in (1, 2, 3):
-        first_cell = 2 + offset if dim_pos == axis_pos else 2
-        result = lax.slice_in_dim(result, first_cell, first_cell + padded.shape[dim_pos] - 4, axis=dim_pos)
-    return result
-
-
-def laplace_four(padded):
-    summed = centre_weight * shifted(padded, 0, 0)
-    for axis_pos in (1, 2, 3):
-        summed = summed + near_weight * (shifted(padded, axis_pos, 1) + shifted(padded, axis_pos, -1))
-        summed = summed + far_weight * (shifted(padded, axis_pos, 2) + shifted(padded, axis_pos, -2))
-    return summed
+    lax.fori_loop(0, STEPS, one_step, 0)
+    prior_ref[...] = held[STEPS] + driven[STEPS - 1]
+    final_ref[...] = held[STEPS + 1] + driven[STEPS]
 
 
 def local(current_field, earlier_field, wave_coef, layer_mask, point_xyz, point_owner, cell_offset, wave_vector, frequency, amplitude, phase_index, phase_table):
-    devices = lax.axis_size("slab") * lax.axis_size("comp")
+    slabs, in_group = lax.axis_size("slab"), lax.axis_size("comp")
+    in_row = min(8, slabs // 2)
+    in_column = slabs // in_row
+    devices = slabs * in_group
     points = point_xyz.shape[1]
     width = frequency.shape[0]
-    weight, column = mode_tables()
-    send, own = pl.pallas_call(
-        pack_kernel,
-        out_shape=(
-            jax.ShapeDtypeStruct((devices, 4 * SLOTS), F32),
-            jax.ShapeDtypeStruct((8, width), F32),
-        ),
-        compiler_params=pltpu.CompilerParams(vmem_limit_bytes=48 << 20),
-    )(
-        point_owner.reshape(1, points), point_xyz, cell_offset.reshape(1, points), wave_vector,
-        frequency.reshape(1, width), amplitude, phase_index.reshape(1, width), phase_table.reshape(-1, 1),
-    )
-    got = lax.all_to_all(send, ("slab", "comp"), split_axis=0, concat_axis=0, tiled=True)
-    comps = lax.all_gather(own, "comp", axis=0)
     _, nx, ny, nz = current_field.shape
     modes = 4 * HALF * HALF
     slots = devices * SLOTS
     chunk = 256
-    forcing = pl.pallas_call(
-        incident_kernel,
-        out_shape=jax.ShapeDtypeStruct((FIELDS, nx * ny, nz), F32),
+    weight, column = mode_tables()
+    field = jax.ShapeDtypeStruct(current_field.shape, F32)
+    operands = (
+        current_field, earlier_field, wave_coef, layer_mask, point_owner.reshape(1, points), point_xyz,
+        cell_offset.reshape(1, points), wave_vector, frequency.reshape(1, width), amplitude,
+        phase_index.reshape(1, width), phase_table.reshape(1, -1), jnp.asarray(weight), jnp.asarray(column),
+    )
+    like = [pltpu.VMEM(a.shape, a.dtype) for a in operands]
+    dma = pltpu.SemaphoreType.DMA
+    exchanges = 2 * STEPS - 1
+    final_field, prior_field = pl.pallas_call(
+        functools.partial(wave_kernel, (in_row, in_column, in_group)),
+        out_shape=(field, field),
+        in_specs=[pl.BlockSpec(memory_space=pl.ANY)] * len(operands),
+        out_specs=[pl.BlockSpec(memory_space=pltpu.VMEM)] * 2,
         scratch_shapes=[
+            pltpu.VMEM((STEPS + 2, 3, nx, ny, nz), F32),
+            pltpu.VMEM((STEPS + 1, 3, nx, ny, nz), F32),
+            like[2], like[3], pltpu.VMEM((nx, ny, nz), F32), *like[4:], dma((len(operands),)),
+            pltpu.VMEM((in_group, 8, width), F32), dma((in_group,)), dma((in_group,)),
+            pltpu.VMEM((in_row, in_column, in_group, 1, 4 * SLOTS), F32),
+            pltpu.VMEM((in_row, in_column, in_group, 1, 4 * SLOTS), F32),
+            pltpu.VMEM((in_column, in_row, in_group, 1, 4 * SLOTS), F32),
+            pltpu.VMEM((in_group, in_column, in_row, 1, 4 * SLOTS), F32),
+            dma((3, in_row)), dma((3, in_row)), dma((3,)),
+            pltpu.VMEM((exchanges, 2, 3, 2, ny, nz), F32),
+            pltpu.VMEM((exchanges, 2, 3, nx, 2, nz), F32),
+            pltpu.VMEM((exchanges, 2, 3, nx, 2, nz), F32),
+            dma((exchanges, 4)), dma((exchanges, 4)),
             pltpu.VMEM((2, FIELDS * MODES, width), BF16),
             pltpu.VMEM((2, FIELDS * MODES, width), BF16),
             pltpu.VMEM((2, modes // 2, width), BF16),
@@ -284,21 +476,13 @@
             pltpu.VMEM((modes, chunk), BF16),
             pltpu.VMEM((FIELDS, slots), F32),
             pltpu.VMEM((nz, slots), BF16),
+            pltpu.VMEM((3, nx * ny, nz), F32),
         ],
-        compiler_params=pltpu.CompilerParams(vmem_limit_bytes=48 << 20),
-    )(got, comps, jnp.asarray(weight), jnp.asarray(column))
-    forcing = forcing.reshape(FIELDS, nx, ny, nz)
-    sign_field = ((layer_mask == 1).astype(F32) - (layer_mask == 2).astype(F32))[None]
-    current = current_field
-    earlier = earlier_field
-    for step_index in range(STEPS):
-        widened = with_halo(current, (("slab", 1), ("comp", 2)), 2)
-        padded = jnp.pad(widened, ((0, 0), (0, 0), (0, 0), (2, 2)))
-        source = forcing[3 * step_index : 3 * step_index + 3]
-        following = 2.0 * current - earlier + wave_coef[None] * laplace_four(padded) + sign_field * source
-        earlier = current
-        current = following
-    return (current, earlier)
+        compiler_params=pltpu.CompilerParams(
+            collective_id=0, has_side_effects=True, vmem_limit_bytes=60 << 20
+        ),
+    )(*operands)
+    return final_field, prior_field
 
 
 def solution(mesh):

time: 124 us -> 61.3 us (0.49)
  the two profiles are of different devices: /device:TPU:25 before, /device:TPU:0 now
where the time goes in v2:
time: 61.3 us; the launch traced here: 61.1 us
  Pallas kernels  57.9 us (94%)
  local copies, waits for them, and re-layouts  2.57 us (4%)
  between operations  0.65 us (1%)
    pallas_call x1, Pallas kernels, local(): pl.pallas_call(functools.partial(wave_kernel, (in_row, in_column, in_grou...  57.9 us
    unnamed x4, local copies, waits for them, and re-layouts  2.57 us

profile of v2, /device:TPU:0, one launch (start us, length us, event | category | flops | bytes accessed | tf_op | source)
XLA Modules:
  0.0 61.1 jit_solution(10086825890417730032)
XLA Ops:
  0.6 57.9 %shard_map.149 = (f32[3,8,16,256]{3,2,1,0:T(8,128)}, f32[3,8,16,256]{3,2,1,0:T(8,128)}) custom-call(f32[3,8,16,256]{3,2,1,0:T(8,128)} %current_in.1, f32[3,8,16,256]{3,2,1,0:T(8,128)} %earlier_in.1, f32[8,16,256]{2,1,0:T(8,128)} %coef_in.1, s32[8,16,256]{2,1,0:T(8,128)} %mask_in.1, s32[1,1024]{1,0:T(1,128)} %bitcast.5, f32[3,1024]{1,0:T(4,128)} %xyz_in.1, ...), custom_call_target="tpu_custom_call" | custom-call | tf_op jit(solution)/shard_map/pallas_call | solution.py:448
  58.6 0.0 copy-start
  58.6 1.8 %copy.18 = f32[3,8,16,256]{3,2,1,0:T(8,128)} copy(f32[3,8,16,256]{3,2,1,0:T(8,128)} %get-tuple-element.4) | data formatting | bytes 786432
  60.4 0.0 copy-done
  60.4 0.7 %copy.19 = f32[3,8,16,256]{3,2,1,0:T(8,128)} copy(f32[3,8,16,256]{3,2,1,0:T(8,128)S(1)} %copy-done) | data formatting | bytes 786432
Async XLA Ops:
  58.6 1.8 %copy-start = (f32[3,8,16,256]{3,2,1,0:T(8,128)S(1)}, f32[3,8,16,256]{3,2,1,0:T(8,128)}, u32[]{:S(2)}) copy-start(f32[3,8,16,256]{3,2,1,0:T(8,128)} %get-tuple-element.5) | copy-start | bytes 1179652

commit v3 on v2

--- a/solution.py
+++ b/solution.py
@@ -80,9 +80,9 @@
     return lax.dot_general(a, b, (((1,), (0,)), ((), ())), preferred_element_type=F32)
 
 
-def mode_sums(block, weight, column, q_hi, q_lo, p_hi, p_lo):
-    width = block.shape[1]
+def mode_sums(block, weight, column, odd, q, p_hi, p_lo):
     turn = 1.0 / (2.0 * np.pi)
+    rows = FIELDS * MODES
     angles = jnp.concatenate(
         [column[d * HALF : (d + 1) * HALF, 0:1] * (block[d : d + 1, :] * (2.0 * turn)) for d in range(3)], axis=0
     )
@@ -95,26 +95,26 @@
     centre = (2.0 * turn) * (block[0:1, :] + block[1:2, :] + block[2:3, :]) + turn * block[7:8, :]
     for n in range(STEPS):
         shift_cos, shift_sin = cos_sin_turns(centre - block[3:4, :] * (turn * step_size * (n + 1)))
+        outer = jnp.where(odd, -shift_sin, shift_cos)
+        inner = jnp.where(odd, -shift_cos, -shift_sin)
         for i in range(3):
-            b = block[4 + i : 5 + i, :] * shift_cos
-            c = -block[4 + i : 5 + i, :] * shift_sin
+            amp = block[4 + i : 5 + i, :]
             at = (3 * n + i) * MODES
-            for which, part, value in ((0, 0, b * cz), (0, 1, c * sz), (1, 0, c * cz), (1, 1, -(b * sz))):
-                rows = pl.ds(at + part * HALF, HALF)
-                q_hi[which, rows, :], q_lo[which, rows, :] = split2(value)
+            for part, value in ((0, (amp * outer) * cz), (1, (amp * inner) * sz)):
+                low = at + part * HALF
+                q[low : low + HALF, :], q[rows + low : rows + low + HALF, :] = split2(value)
+    even_y = jnp.where(odd, sy, cy)
+    odd_y = jnp.where(odd, cy, -sy)
     for m in range(HALF):
         rows_a, rows_b = pl.ds(m * HALF, HALF), pl.ds((HALF + m) * HALF, HALF)
-        x_even, x_odd = cx[m : m + 1, :], sx[m : m + 1, :]
-        p_hi[0, rows_a, :], p_lo[0, rows_a, :] = split2(x_even * cy)
-        p_hi[0, rows_b, :], p_lo[0, rows_b, :] = split2(-(x_odd * sy))
-        p_hi[1, rows_a, :], p_lo[1, rows_a, :] = split2(x_even * sy)
-        p_hi[1, rows_b, :], p_lo[1, rows_b, :] = split2(x_odd * cy)
-
-
-def mode_products(q_hi, q_lo, p_hi, p_lo, which):
-    return (
-        dot_nt(q_hi[which], p_hi[which]) + dot_nt(q_hi[which], p_lo[which]) + dot_nt(q_lo[which], p_hi[which])
-    )
+        p_hi[rows_a, :], p_lo[rows_a, :] = split2(cx[m : m + 1, :] * even_y)
+        p_hi[rows_b, :], p_lo[rows_b, :] = split2(sx[m : m + 1, :] * odd_y)
+
+
+def mode_products(q, p_hi, p_lo):
+    rows = FIELDS * MODES
+    both = dot_nt(q[...], p_hi[...])
+    return both[:rows] + both[rows:] + dot_nt(q[:rows, :], p_lo[...])
 
 
 def slot_rows(arrived):
@@ -135,7 +135,7 @@
         older, old = old, 2.0 * tau * old - older
 
 
-def point_sums(t_ref, lanes, f_hi, f_lo, w_hi, w_lo, v_ref):
+def point_sums(t_ref, lanes, f, w_hi, w_lo, v_ref):
     tx, ty, tz = t_ref[0, :, lanes], t_ref[1, :, lanes], t_ref[2, :, lanes]
     half = [slice(0, HALF), slice(HALF, MODES)]
     for combo, (px, py) in enumerate(((0, 0), (1, 1), (0, 1), (1, 0))):
@@ -144,15 +144,36 @@
             rows = pl.ds((combo * HALF + m) * HALF, HALF)
             at = px * HALF + m
             w_hi[rows, :], w_lo[rows, :] = split2(tx[at : at + 1, :] * other)
-    sums = dot_nn(f_hi[...], w_hi[...]) + dot_nn(f_hi[...], w_lo[...]) + dot_nn(f_lo[...], w_hi[...])
+    count = FIELDS * MODES
+    both = dot_nn(f[...], w_hi[...])
+    sums = both[:count] + both[count:] + dot_nn(f[:count, :], w_lo[...])
     for j in range(FIELDS):
-        v_ref[j : j + 1, lanes] = jnp.sum(sums[j * MODES : (j + 1) * MODES, :] * tz, axis=0, keepdims=True)
-
-
-def spread_field(v, place, z_hot, cells_xy):
-    hit = place == lax.broadcasted_iota(jnp.int32, (cells_xy, place.shape[1]), 0).astype(F32)
-    v_hi, v_lo = split2(jnp.where(hit, v, 0.0))
-    return dot_nt(v_hi, z_hot) + dot_nt(v_lo, z_hot)
+        v_ref[j // 3, j % 3 : j % 3 + 1, lanes] = jnp.sum(sums[j * MODES : (j + 1) * MODES, :] * tz, axis=0, keepdims=True)
+
+
+def hot_rows(arrived, cell, xy_hot, z_hot):
+    depth = z_hot.shape[1]
+    place = jnp.floor((cell - 1.0) * (1.0 / depth))
+    xy_hot[...] = jnp.where(
+        place == lax.broadcasted_iota(jnp.int32, xy_hot.shape, 0).astype(F32), 1.0, 0.0
+    ).astype(BF16)
+    sources = arrived.shape[0]
+    lane = lax.broadcasted_iota(jnp.int32, (sources, depth), 1).astype(F32)
+    for r in range(SLOTS):
+        one = arrived[:, 3 * SLOTS + r : 3 * SLOTS + r + 1] - 1.0
+        along = one - jnp.floor(one * (1.0 / depth)) * depth
+        z_hot[r * sources : (r + 1) * sources, :] = jnp.where(along == lane, 1.0, 0.0).astype(BF16)
+
+
+def spread_fields(v, xy_hot, z_hot, spread, forcing):
+    cells = xy_hot.shape[0]
+    v_hi, v_lo = split2(v)
+    for i in range(3):
+        spread[2 * i * cells : (2 * i + 1) * cells, :] = xy_hot[...] * v_hi[i : i + 1, :]
+        spread[(2 * i + 1) * cells : (2 * i + 2) * cells, :] = xy_hot[...] * v_lo[i : i + 1, :]
+    total = dot_nn(spread[...], z_hot[...])
+    for i in range(3):
+        forcing[i] = total[2 * i * cells : (2 * i + 1) * cells] + total[(2 * i + 1) * cells : (2 * i + 2) * cells]
 
 
 def pack_points(owner, xyz, offset, send, split):
@@ -186,12 +207,12 @@
     split,
     current_in, earlier_in, coef_in, mask_in, owner_in, xyz_in, offset_in, wave_in, freq_in, amp_in, index_in, table_in,
     weight_in, column_in,
-    final_ref, prior_ref,
+    held_out, driven_out,
     held, driven, coef, mask, sign, owner, xyz, offset, wave, freq, amp, index, table, weight, column, load_sem,
     comps, comp_send, comp_recv,
     sent, first, second, third, hop_send, hop_recv, hop_own,
     x_in, y_in, y_out, halo_send, halo_recv,
-    q_hi, q_lo, p_hi, p_lo, f_ref, f_hi, f_lo, t_ref, w_hi, w_lo, v_ref, z_hot, forcing,
+    q, p_hi, p_lo, f_ref, f_send, f_recv, f, t_ref, w_hi, w_lo, v_ref, xy_hot, z_hot, spread, forcing, store_sem,
 ):
     in_row, in_column, in_group = split
     slabs = in_row * in_column
@@ -341,16 +362,25 @@
         lax.fori_loop(0, 3, one, 0)
 
     wide = 2 * HALF * HALF
-    f_ref[...] = jnp.zeros_like(f_ref)
+    core = lax.rem(comp, 2)
+    odd = core == 1
+    stores = [
+        pltpu.make_async_copy(a, b, store_sem.at[i])
+        for i, (a, b) in enumerate((
+            (held.at[pl.ds(STEPS, 2)], held_out),
+            (driven.at[STEPS - 1], driven_out.at[0]),
+            (driven.at[STEPS], driven_out.at[1]),
+        ))
+    ]
+    f_ref[core] = jnp.zeros((FIELDS * MODES, wide), F32)
 
     def one_block(i, carry):
         @pl.when(i > 0)
         def _():
             comp_copy(i).wait()
 
-        mode_sums(comps[i], weight[...], column[...], q_hi, q_lo, p_hi, p_lo)
-        for which in (0, 1):
-            f_ref[:, which * wide : (which + 1) * wide] += mode_products(q_hi, q_lo, p_hi, p_lo, which)
+        mode_sums(comps[i], weight[...], column[...], odd, q, p_hi, p_lo)
+        f_ref[core] += mode_products(q, p_hi, p_lo)
 
         for hop in (0, 1):
             @pl.when(i == hop)
@@ -370,31 +400,37 @@
         return carry
 
     lax.fori_loop(0, in_group, one_block, 0)
-    f_hi[...], f_lo[...] = split2(f_ref[...])
+    half_copy = pltpu.make_async_remote_copy(
+        src_ref=f_ref.at[core], dst_ref=f_ref.at[core], send_sem=f_send, recv_sem=f_recv,
+        device_id=(slab, comp + 1 - 2 * core), device_id_type=MESH,
+    )
+    half_copy.start()
+    stores[0].start()
     wait_hop(2)
-    px, py, pz, cell = slot_rows(third[...].reshape(in_group * slabs, 4 * SLOTS))
+    arrived = third[...].reshape(in_group * slabs, 4 * SLOTS)
+    px, py, pz, cell = slot_rows(arrived)
     point_modes([px, py, pz], t_ref)
+    hot_rows(arrived, cell, xy_hot, z_hot)
+    half_copy.wait()
+    rows = FIELDS * MODES
+    for which in (0, 1):
+        lanes = pl.ds(which * wide, wide)
+        f[:rows, lanes], f[rows:, lanes] = split2(f_ref[which])
     chunk = w_hi.shape[1]
 
     def one_chunk(i, carry):
-        point_sums(t_ref, pl.ds(pl.multiple_of(i * chunk, chunk), chunk), f_hi, f_lo, w_hi, w_lo, v_ref)
+        point_sums(t_ref, pl.ds(pl.multiple_of(i * chunk, chunk), chunk), f, w_hi, w_lo, v_ref)
         return carry
 
     lax.fori_loop(0, t_ref.shape[2] // chunk, one_chunk, 0)
-    place = jnp.floor((cell - 1.0) * (1.0 / nz))
-    along = (cell - 1.0) - place * nz
-    z_hot[...] = jnp.where(
-        along == lax.broadcasted_iota(jnp.int32, z_hot.shape, 0).astype(F32), 1.0, 0.0
-    ).astype(BF16)
     driven[0] = jnp.zeros_like(driven[0])
 
     def one_step(n, carry):
-        def one_field(i, inner):
-            j = 3 * n + i
-            forcing[i] = spread_field(v_ref[pl.ds(j, 1), :], place, z_hot[...], nx * ny)
-            return inner
-
-        lax.fori_loop(0, 3, one_field, 0)
+        @pl.when(n == STEPS - 1)
+        def _():
+            stores[1].start()
+
+        spread_fields(v_ref[n], xy_hot, z_hot, spread, forcing)
 
         def source(c, x):
             return sign[x] * forcing[c, x * ny : (x + 1) * ny, :]
@@ -420,8 +456,9 @@
         return carry
 
     lax.fori_loop(0, STEPS, one_step, 0)
-    prior_ref[...] = held[STEPS] + driven[STEPS - 1]
-    final_ref[...] = held[STEPS + 1] + driven[STEPS]
+    stores[2].start()
+    for store in stores:
+        store.wait()
 
 
 def local(current_field, earlier_field, wave_coef, layer_mask, point_xyz, point_owner, cell_offset, wave_vector, frequency, amplitude, phase_index, phase_table):
@@ -436,7 +473,7 @@
     slots = devices * SLOTS
     chunk = 256
     weight, column = mode_tables()
-    field = jax.ShapeDtypeStruct(current_field.shape, F32)
+    pair = jax.ShapeDtypeStruct((2, *current_field.shape), F32)
     operands = (
         current_field, earlier_field, wave_coef, layer_mask, point_owner.reshape(1, points), point_xyz,
         cell_offset.reshape(1, points), wave_vector, frequency.reshape(1, width), amplitude,
@@ -445,11 +482,11 @@
     like = [pltpu.VMEM(a.shape, a.dtype) for a in operands]
     dma = pltpu.SemaphoreType.DMA
     exchanges = 2 * STEPS - 1
-    final_field, prior_field = pl.pallas_call(
+    held, driven = pl.pallas_call(
         functools.partial(wave_kernel, (in_row, in_column, in_group)),
-        out_shape=(field, field),
+        out_shape=(pair, pair),
         in_specs=[pl.BlockSpec(memory_space=pl.ANY)] * len(operands),
-        out_specs=[pl.BlockSpec(memory_space=pltpu.VMEM)] * 2,
+        out_specs=[pl.BlockSpec(memory_space=pl.ANY)] * 2,
         scratch_shapes=[
             pltpu.VMEM((STEPS + 2, 3, nx, ny, nz), F32),
             pltpu.VMEM((STEPS + 1, 3, nx, ny, nz), F32),
@@ -464,25 +501,25 @@
             pltpu.VMEM((exchanges, 2, 3, nx, 2, nz), F32),
             pltpu.VMEM((exchanges, 2, 3, nx, 2, nz), F32),
             dma((exchanges, 4)), dma((exchanges, 4)),
-            pltpu.VMEM((2, FIELDS * MODES, width), BF16),
-            pltpu.VMEM((2, FIELDS * MODES, width), BF16),
-            pltpu.VMEM((2, modes // 2, width), BF16),
-            pltpu.VMEM((2, modes // 2, width), BF16),
-            pltpu.VMEM((FIELDS * MODES, modes), F32),
-            pltpu.VMEM((FIELDS * MODES, modes), BF16),
-            pltpu.VMEM((FIELDS * MODES, modes), BF16),
+            pltpu.VMEM((2 * FIELDS * MODES, width), BF16),
+            pltpu.VMEM((modes // 2, width), BF16),
+            pltpu.VMEM((modes // 2, width), BF16),
+            pltpu.VMEM((2, FIELDS * MODES, modes // 2), F32), dma, dma,
+            pltpu.VMEM((2 * FIELDS * MODES, modes), BF16),
             pltpu.VMEM((3, MODES, slots), F32),
             pltpu.VMEM((modes, chunk), BF16),
             pltpu.VMEM((modes, chunk), BF16),
-            pltpu.VMEM((FIELDS, slots), F32),
-            pltpu.VMEM((nz, slots), BF16),
-            pltpu.VMEM((3, nx * ny, nz), F32),
+            pltpu.VMEM((STEPS, 3, slots), F32),
+            pltpu.VMEM((nx * ny, slots), BF16),
+            pltpu.VMEM((slots, nz), BF16),
+            pltpu.VMEM((6 * nx * ny, slots), BF16),
+            pltpu.VMEM((3, nx * ny, nz), F32), dma((3,)),
         ],
         compiler_params=pltpu.CompilerParams(
             collective_id=0, has_side_effects=True, vmem_limit_bytes=60 << 20
         ),
     )(*operands)
-    return final_field, prior_field
+    return held[1] + driven[1], held[0] + driven[0]
 
 
 def solution(mesh):

time: 61.3 us -> 60.4 us (0.985)
  local copies, waits for them, and re-layouts: 2.57 us -> 0 us
  other arithmetic: 0 us -> 2.37 us
  Pallas kernels: 57.9 us -> 57.2 us
    unnamed x4 -> x0, local copies, waits for them, and re-layouts: 2.57 us -> none
    add x0 -> x1, other arithmetic: none -> 2.37 us  [local(): return (held[1] + driven[1], held[0] + driven[0])]
    pallas_call x1, Pallas kernels: 57.9 us -> 57.2 us  [local(): pl.pallas_call(functools.partial(wave_kernel, (in_row, in_column, in_grou...]
where the time goes in v3:
time: 60.4 us; the launch traced here: 60.2 us
  Pallas kernels  57.2 us (95%)
  other arithmetic  2.37 us (4%)
  between operations  0.64 us (1%)
    pallas_call x1, Pallas kernels, local(): pl.pallas_call(functools.partial(wave_kernel, (in_row, in_column, in_grou...  57.2 us
    add x1, other arithmetic, local(): return (held[1] + driven[1], held[0] + driven[0])  2.37 us

profile of v3, /device:TPU:0, one launch (start us, length us, event | category | flops | bytes accessed | tf_op | source)
XLA Modules:
  0.0 60.2 jit_solution(2729068572293880201)
XLA Ops:
  0.6 57.2 %shard_map.149 = (f32[2,3,8,16,256]{4,3,2,1,0:T(8,128)}, f32[2,3,8,16,256]{4,3,2,1,0:T(8,128)}) custom-call(f32[3,8,16,256]{3,2,1,0:T(8,128)} %current_in.1, f32[3,8,16,256]{3,2,1,0:T(8,128)} %earlier_in.1, f32[8,16,256]{2,1,0:T(8,128)} %coef_in.1, s32[8,16,256]{2,1,0:T(8,128)} %mask_in.1, s32[1,1024]{1,0:T(1,128)} %bitcast.9, f32[3,1024]{1,0:T(4,128)} %xyz_in.1, ...), custom_call_target="tpu_custom_call" | custom-call | tf_op jit(solution)/shard_map/pallas_call | solution.py:485
  57.9 2.4 %add_bitcast_fusion = (f32[3,8,16,256]{3,2,1,0:T(8,128)}, f32[3,8,16,256]{3,2,1,0:T(8,128)}) fusion(f32[2,3,8,16,256]{4,3,2,1,0:T(8,128)} %get-tuple-element.5, f32[2,3,8,16,256]{4,3,2,1,0:T(8,128)} %get-tuple-element.4), kind=kLoop, calls=%fused_computation | loop fusion | flops 196608 | bytes 2359296 | tf_op jit(solution)/shard_map/add | solution.py:522

commit v4 on v3

--- a/solution.py
+++ b/solution.py
@@ -207,12 +207,12 @@
     split,
     current_in, earlier_in, coef_in, mask_in, owner_in, xyz_in, offset_in, wave_in, freq_in, amp_in, index_in, table_in,
     weight_in, column_in,
-    held_out, driven_out,
+    final_ref, prior_ref,
     held, driven, coef, mask, sign, owner, xyz, offset, wave, freq, amp, index, table, weight, column, load_sem,
     comps, comp_send, comp_recv,
     sent, first, second, third, hop_send, hop_recv, hop_own,
     x_in, y_in, y_out, halo_send, halo_recv,
-    q, p_hi, p_lo, f_ref, f_send, f_recv, f, t_ref, w_hi, w_lo, v_ref, xy_hot, z_hot, spread, forcing, store_sem,
+    q, p_hi, p_lo, f_ref, f_send, f_recv, f, t_ref, w_hi, w_lo, v_ref, xy_hot, z_hot, spread, forcing,
 ):
     in_row, in_column, in_group = split
     slabs = in_row * in_column
@@ -364,14 +364,6 @@
     wide = 2 * HALF * HALF
     core = lax.rem(comp, 2)
     odd = core == 1
-    stores = [
-        pltpu.make_async_copy(a, b, store_sem.at[i])
-        for i, (a, b) in enumerate((
-            (held.at[pl.ds(STEPS, 2)], held_out),
-            (driven.at[STEPS - 1], driven_out.at[0]),
-            (driven.at[STEPS], driven_out.at[1]),
-        ))
-    ]
     f_ref[core] = jnp.zeros((FIELDS * MODES, wide), F32)
 
     def one_block(i, carry):
@@ -383,19 +375,16 @@
         f_ref[core] += mode_products(q, p_hi, p_lo)
 
         for hop in (0, 1):
-            @pl.when(i == hop)
+            @pl.when(i == 2 * hop + 1)
             def _(hop=hop):
                 wait_hop(hop)
                 start_hop(hop + 1)
 
-        @pl.when(i < STEPS)
+        @pl.when(i == 2)
         def _():
-            wait_halo(i, held.at[i + 1])
-            advance(i, held, i, None)
-
-            @pl.when(i < STEPS - 1)
-            def _():
-                start_halo(i + 1, held.at[i + 2])
+            wait_halo(0, held.at[1])
+            advance(0, held, 0, None)
+            start_halo(1, held.at[2])
 
         return carry
 
@@ -405,7 +394,6 @@
         device_id=(slab, comp + 1 - 2 * core), device_id_type=MESH,
     )
     half_copy.start()
-    stores[0].start()
     wait_hop(2)
     arrived = third[...].reshape(in_group * slabs, 4 * SLOTS)
     px, py, pz, cell = slot_rows(arrived)
@@ -428,7 +416,7 @@
     def one_step(n, carry):
         @pl.when(n == STEPS - 1)
         def _():
-            stores[1].start()
+            prior_ref[...] = held[STEPS] + driven[STEPS - 1]
 
         spread_fields(v_ref[n], xy_hot, z_hot, spread, forcing)
 
@@ -452,13 +440,17 @@
         @pl.when(n < STEPS - 1)
         def _():
             start_halo(STEPS + n, driven.at[n + 1])
+            wait_halo(n + 1, held.at[n + 2])
+            advance(n + 1, held, n + 1, None)
+
+            @pl.when(n < STEPS - 2)
+            def _():
+                start_halo(n + 2, held.at[n + 3])
 
         return carry
 
     lax.fori_loop(0, STEPS, one_step, 0)
-    stores[2].start()
-    for store in stores:
-        store.wait()
+    final_ref[...] = held[STEPS + 1] + driven[STEPS]
 
 
 def local(current_field, earlier_field, wave_coef, layer_mask, point_xyz, point_owner, cell_offset, wave_vector, frequency, amplitude, phase_index, phase_table):
@@ -473,7 +465,7 @@
     slots = devices * SLOTS
     chunk = 256
     weight, column = mode_tables()
-    pair = jax.ShapeDtypeStruct((2, *current_field.shape), F32)
+    field = pltpu.VMEM(current_field.shape, F32)
     operands = (
         current_field, earlier_field, wave_coef, layer_mask, point_owner.reshape(1, points), point_xyz,
         cell_offset.reshape(1, points), wave_vector, frequency.reshape(1, width), amplitude,
@@ -482,11 +474,11 @@
     like = [pltpu.VMEM(a.shape, a.dtype) for a in operands]
     dma = pltpu.SemaphoreType.DMA
     exchanges = 2 * STEPS - 1
-    held, driven = pl.pallas_call(
+    final_field, prior_field = pl.pallas_call(
         functools.partial(wave_kernel, (in_row, in_column, in_group)),
-        out_shape=(pair, pair),
+        out_shape=(field, field),
         in_specs=[pl.BlockSpec(memory_space=pl.ANY)] * len(operands),
-        out_specs=[pl.BlockSpec(memory_space=pl.ANY)] * 2,
+        out_specs=[pl.BlockSpec(memory_space=pltpu.VMEM)] * 2,
         scratch_shapes=[
             pltpu.VMEM((STEPS + 2, 3, nx, ny, nz), F32),
             pltpu.VMEM((STEPS + 1, 3, nx, ny, nz), F32),
@@ -513,13 +505,13 @@
             pltpu.VMEM((nx * ny, slots), BF16),
             pltpu.VMEM((slots, nz), BF16),
             pltpu.VMEM((6 * nx * ny, slots), BF16),
-            pltpu.VMEM((3, nx * ny, nz), F32), dma((3,)),
+            pltpu.VMEM((3, nx * ny, nz), F32),
         ],
         compiler_params=pltpu.CompilerParams(
-            collective_id=0, has_side_effects=True, vmem_limit_bytes=60 << 20
+            collective_id=0, has_side_effects=True, vmem_limit_bytes=60400 << 10
         ),
     )(*operands)
-    return held[1] + driven[1], held[0] + driven[0]
+    return final_field, prior_field
 
 
 def solution(mesh):

time: 60.4 us -> 51.2 us (0.85)
  the two profiles are of different devices: /device:TPU:0 before, /device:TPU:1 now
where the time goes in v4:
time: 51.2 us; the launch traced here: 51.1 us
  Pallas kernels  48.9 us (96%)
  local copies, waits for them, and re-layouts  1.49 us (3%)
  between operations  0.64 us (1%)
    pallas_call x1, Pallas kernels, local(): pl.pallas_call(functools.partial(wave_kernel, (in_row, in_column, in_grou...  48.9 us
    unnamed x2, local copies, waits for them, and re-layouts  1.49 us

profile of v4, /device:TPU:1, one launch (start us, length us, event | category | flops | bytes accessed | tf_op | source)
XLA Modules:
  0.0 51.1 jit_solution(13527659801553032872)
XLA Ops:
  0.6 48.9 %shard_map.149 = (f32[3,8,16,256]{3,2,1,0:T(8,128)S(1)}, f32[3,8,16,256]{3,2,1,0:T(8,128)S(1)}) custom-call(f32[3,8,16,256]{3,2,1,0:T(8,128)} %current_in.1, f32[3,8,16,256]{3,2,1,0:T(8,128)} %earlier_in.1, f32[8,16,256]{2,1,0:T(8,128)} %coef_in.1, s32[8,16,256]{2,1,0:T(8,128)} %mask_in.1, s32[1,1024]{1,0:T(1,128)} %bitcast.5, f32[3,1024]{1,0:T(4,128)} %xyz_in.1, ...), custom_call_target="tpu_custom_call" | custom-call | tf_op jit(solution)/shard_map/pallas_call | solution.py:477
  49.6 0.7 %copy.18 = f32[3,8,16,256]{3,2,1,0:T(8,128)} copy(f32[3,8,16,256]{3,2,1,0:T(8,128)S(1)} %get-tuple-element.2) | data formatting | bytes 786432
  50.3 0.7 %copy.19 = f32[3,8,16,256]{3,2,1,0:T(8,128)} copy(f32[3,8,16,256]{3,2,1,0:T(8,128)S(1)} %get-tuple-element.3) | data formatting | bytes 786432

commit v5 on v4

--- a/solution.py
+++ b/solution.py
@@ -135,20 +135,24 @@
         older, old = old, 2.0 * tau * old - older
 
 
-def point_sums(t_ref, lanes, f, w_hi, w_lo, v_ref):
-    tx, ty, tz = t_ref[0, :, lanes], t_ref[1, :, lanes], t_ref[2, :, lanes]
+def point_products(t_ref, lanes, w_hi, w_lo):
+    tx, ty = t_ref[0, :, lanes], t_ref[1, :, lanes]
     half = [slice(0, HALF), slice(HALF, MODES)]
     for combo, (px, py) in enumerate(((0, 0), (1, 1), (0, 1), (1, 0))):
         other = ty[half[py], :]
         for m in range(HALF):
             rows = pl.ds((combo * HALF + m) * HALF, HALF)
             at = px * HALF + m
-            w_hi[rows, :], w_lo[rows, :] = split2(tx[at : at + 1, :] * other)
-    count = FIELDS * MODES
-    both = dot_nn(f[...], w_hi[...])
-    sums = both[:count] + both[count:] + dot_nn(f[:count, :], w_lo[...])
-    for j in range(FIELDS):
-        v_ref[j // 3, j % 3 : j % 3 + 1, lanes] = jnp.sum(sums[j * MODES : (j + 1) * MODES, :] * tz, axis=0, keepdims=True)
+            w_hi[rows, lanes], w_lo[rows, lanes] = split2(tx[at : at + 1, :] * other)
+
+
+def point_sums(n, t_ref, lanes, f, w_hi, w_lo, v_ref):
+    tz = t_ref[2, :, lanes]
+    count = 3 * MODES
+    both = dot_nn(f[n], w_hi[:, lanes])
+    sums = both[:count] + both[count:] + dot_nn(f[n, :count, :], w_lo[:, lanes])
+    for i in range(3):
+        v_ref[n, i : i + 1, lanes] = jnp.sum(sums[i * MODES : (i + 1) * MODES, :] * tz, axis=0, keepdims=True)
 
 
 def hot_rows(arrived, cell, xy_hot, z_hot):
@@ -177,64 +181,74 @@
 
 
 def pack_points(owner, xyz, offset, send, split):
-    in_row, in_column, in_group = split
+    in_x, in_z, in_y, in_group = split
     points = owner.shape[1]
-    devices = in_row * in_column * in_group
+    devices = in_x * in_z * in_y * in_group
+    bits = [n.bit_length() - 1 for n in (in_group, in_x, in_z)]
     c = owner & (in_group - 1)
-    slab = owner >> (in_group.bit_length() - 1)
-    w, y = slab & (in_row - 1), slab >> (in_row.bit_length() - 1)
-    place = (w * in_column + y) * in_group + c
+    x = (owner >> bits[0]) & (in_x - 1)
+    z = (owner >> (bits[0] + bits[1])) & (in_z - 1)
+    y = owner >> (bits[0] + bits[1] + bits[2])
+    place = ((y * in_x + x) * in_z + z) * in_group + c
     hit = place == lax.broadcasted_iota(jnp.int32, (devices, points), 0)
     match = jnp.where(hit, 1.0, 0.0)
     match16 = match.astype(BF16)
-    before = (
-        lax.broadcasted_iota(jnp.int32, (points, points), 0)
-        < lax.broadcasted_iota(jnp.int32, (points, points), 1)
-    )
-    count = dot_nn(match16, jnp.where(before, 1.0, 0.0).astype(BF16))
-    rank = jnp.sum(count * match, axis=0, keepdims=True)
+    run = min(points, 128)
+    rows, columns = (lax.broadcasted_iota(jnp.int32, (run, 2 * run), d) for d in (0, 1))
+    before = jnp.where((rows < columns) | (columns >= run), 1.0, 0.0).astype(BF16)
+    offset_in = jnp.zeros((devices, run), F32)
+    ranks = []
+    for at in range(0, points, run):
+        sums = dot_nn(match16[:, at : at + run], before)
+        ranks.append(jnp.sum((sums[:, :run] + offset_in) * match[:, at : at + run], axis=0, keepdims=True))
+        offset_in = offset_in + sums[:, run:]
+    rank = jnp.concatenate(ranks, axis=1)
     slot = rank == lax.broadcasted_iota(jnp.int32, (SLOTS, points), 0).astype(F32)
     values = [xyz[i : i + 1, :] for i in range(3)] + [(offset + 1).astype(F32)]
     spread = jnp.concatenate([jnp.where(slot, v, 0.0) for v in values], axis=0)
     first = spread.astype(BF16)
     second, third = split2(spread - first.astype(F32))
     rows = dot_nt(match16, first) + dot_nt(match16, second) + dot_nt(match16, third)
+    inner = in_z * in_group
     for d in range(devices):
-        send[d // (in_column * in_group), d // in_group % in_column, d % in_group] = rows[d : d + 1, :]
+        send[d // inner, d % inner] = rows[d : d + 1, :]
 
 
 def wave_kernel(
     split,
     current_in, earlier_in, coef_in, mask_in, owner_in, xyz_in, offset_in, wave_in, freq_in, amp_in, index_in, table_in,
     weight_in, column_in,
-    final_ref, prior_ref,
-    held, driven, coef, mask, sign, owner, xyz, offset, wave, freq, amp, index, table, weight, column, load_sem,
+    held, driven,
+    coef, mask, sign, owner, xyz, offset, wave, freq, amp, index, table, weight, column, load_sem,
     comps, comp_send, comp_recv,
-    sent, first, second, third, hop_send, hop_recv, hop_own,
+    sent, first, second, hop_send, hop_recv, hop_own,
     x_in, y_in, y_out, halo_send, halo_recv,
     q, p_hi, p_lo, f_ref, f_send, f_recv, f, t_ref, w_hi, w_lo, v_ref, xy_hot, z_hot, spread, forcing,
 ):
-    in_row, in_column, in_group = split
-    slabs = in_row * in_column
+    in_x, in_z, in_y, in_group = split
+    slabs = in_x * in_z * in_y
     slab, comp = lax.axis_index("slab"), lax.axis_index("comp")
-    y, w = slab // in_row, slab % in_row
+    x, z, y = slab % in_x, slab // in_x % in_z, slab // (in_x * in_z)
     nx, ny, nz = coef.shape
     after, before = lax.rem(slab + 1, slabs), lax.rem(slab + slabs - 1, slabs)
     right, left = lax.rem(comp + 1, in_group), lax.rem(comp + in_group - 1, in_group)
-
-    def row_at(d):
-        return lax.rem(w + d, in_row)
-
-    def column_at(d):
-        return lax.rem(y + d, in_column)
+    outer, inner = y * in_x + x, z * in_group + comp
+    outers, inners = in_y * in_x, in_z * in_group
+
+    def outer_at(d):
+        there = lax.rem(outer + d, outers)
+        return there, ((there // in_x * in_z + z) * in_x + there % in_x, comp)
+
+    def inner_at(d):
+        there = lax.rem(inner + d, inners)
+        return there, ((y * in_z + there // in_group) * in_x + x, there % in_group)
 
     def group_at(d):
         return lax.rem(comp + d, in_group)
 
     barrier = pltpu.get_barrier_semaphore()
-    partners = [(y * in_row + row_at(d), comp) for d in range(1, in_row)]
-    partners += [(column_at(d) * in_row + w, comp) for d in range(1, in_column)]
-    partners += [(slab, group_at(d)) for d in range(1, in_group)]
+    partners = [outer_at(d)[1] for d in range(1, outers)]
+    partners += [inner_at(d)[1] for d in range(1, inners)]
     partners += [(after, comp), (before, comp)]
     for partner in partners:
         pl.semaphore_signal(barrier, inc=1, device_id=partner, device_id_type=MESH)
@@ -299,13 +313,9 @@
 
     def hop_copies(hop):
         if hop == 0:
-            moves = [(sent.at[row_at(d)], first.at[w], (y * in_row + row_at(d), comp)) for d in range(in_row)]
-        elif hop == 1:
-            moves = [
-                (first.at[:, column_at(d)], second.at[y], (column_at(d) * in_row + w, comp)) for d in range(in_column)
-            ]
+            moves = [(sent.at[outer_at(d)[0]], first.at[outer], outer_at(d)[1]) for d in range(outers)]
         else:
-            moves = [(second.at[:, :, group_at(d)], third.at[comp], (slab, group_at(d))) for d in range(in_group)]
+            moves = [(first.at[:, inner_at(d)[0]], second.at[inner], inner_at(d)[1]) for d in range(inners)]
         own = pltpu.make_async_copy(moves[0][0], moves[0][1], hop_own.at[hop])
         return [own] + [
             pltpu.make_async_remote_copy(
@@ -324,9 +334,9 @@
             copy.wait()
 
     pl.semaphore_wait(barrier, len(partners))
+    start_hop(0)
     for d in range(1, in_group):
         comp_copy(d).start()
-    start_hop(0)
     start_halo(0, held.at[1])
     for load in loads[9:]:
         load.wait()
@@ -374,17 +384,10 @@
         mode_sums(comps[i], weight[...], column[...], odd, q, p_hi, p_lo)
         f_ref[core] += mode_products(q, p_hi, p_lo)
 
-        for hop in (0, 1):
-            @pl.when(i == 2 * hop + 1)
-            def _(hop=hop):
-                wait_hop(hop)
-                start_hop(hop + 1)
-
-        @pl.when(i == 2)
-        def _():
-            wait_halo(0, held.at[1])
-            advance(0, held, 0, None)
-            start_halo(1, held.at[2])
+        @pl.when(i == 1)
+        def _():
+            wait_hop(0)
+            start_hop(1)
 
         return carry
 
@@ -394,30 +397,48 @@
         device_id=(slab, comp + 1 - 2 * core), device_id_type=MESH,
     )
     half_copy.start()
-    wait_hop(2)
-    arrived = third[...].reshape(in_group * slabs, 4 * SLOTS)
+    wait_halo(0, held.at[1])
+    advance(0, held, 0, None)
+    start_halo(1, held.at[2])
+    wait_hop(1)
+    arrived = second[...].reshape(slabs * in_group, 4 * SLOTS)
     px, py, pz, cell = slot_rows(arrived)
     point_modes([px, py, pz], t_ref)
     hot_rows(arrived, cell, xy_hot, z_hot)
+    chunk = 256
+
+    def lanes_of(i):
+        return pl.ds(pl.multiple_of(i * chunk, chunk), chunk)
+
+    def one_product(i, carry):
+        point_products(t_ref, lanes_of(i), w_hi, w_lo)
+        return carry
+
+    chunks = t_ref.shape[2] // chunk
+    lax.fori_loop(0, chunks, one_product, 0)
     half_copy.wait()
-    rows = FIELDS * MODES
+    rows = 3 * MODES
     for which in (0, 1):
         lanes = pl.ds(which * wide, wide)
-        f[:rows, lanes], f[rows:, lanes] = split2(f_ref[which])
-    chunk = w_hi.shape[1]
-
-    def one_chunk(i, carry):
-        point_sums(t_ref, pl.ds(pl.multiple_of(i * chunk, chunk), chunk), f, w_hi, w_lo, v_ref)
-        return carry
-
-    lax.fori_loop(0, t_ref.shape[2] // chunk, one_chunk, 0)
+        for n in range(STEPS):
+            f[n, :rows, lanes], f[n, rows:, lanes] = split2(f_ref[which, n * rows : (n + 1) * rows, :])
     driven[0] = jnp.zeros_like(driven[0])
 
     def one_step(n, carry):
-        @pl.when(n == STEPS - 1)
-        def _():
-            prior_ref[...] = held[STEPS] + driven[STEPS - 1]
-
+        @pl.when(n > 0)
+        def _():
+            wait_halo(n, held.at[n + 1])
+            advance(n, held, n, None)
+
+        @pl.when((n > 0) & (n < STEPS - 1))
+        def _():
+            start_halo(n + 1, held.at[n + 2])
+
+        def one_chunk(i, inner):
+            point_sums(n, t_ref, lanes_of(i), f, w_hi, w_lo, v_ref)
+            return inner
+
+        lax.fori_loop(0, chunks, one_chunk, 0)
         spread_fields(v_ref[n], xy_hot, z_hot, spread, forcing)
 
         def source(c, x):
@@ -440,32 +461,22 @@
         @pl.when(n < STEPS - 1)
         def _():
             start_halo(STEPS + n, driven.at[n + 1])
-            wait_halo(n + 1, held.at[n + 2])
-            advance(n + 1, held, n + 1, None)
-
-            @pl.when(n < STEPS - 2)
-            def _():
-                start_halo(n + 2, held.at[n + 3])
 
         return carry
 
     lax.fori_loop(0, STEPS, one_step, 0)
-    final_ref[...] = held[STEPS + 1] + driven[STEPS]
-
 
 def local(current_field, earlier_field, wave_coef, layer_mask, point_xyz, point_owner, cell_offset, wave_vector, frequency, amplitude, phase_index, phase_table):
     slabs, in_group = lax.axis_size("slab"), lax.axis_size("comp")
-    in_row = min(8, slabs // 2)
-    in_column = slabs // in_row
+    in_x, in_z = 4, 2
+    in_y = slabs // (in_x * in_z)
     devices = slabs * in_group
     points = point_xyz.shape[1]
     width = frequency.shape[0]
     _, nx, ny, nz = current_field.shape
     modes = 4 * HALF * HALF
     slots = devices * SLOTS
-    chunk = 256
     weight, column = mode_tables()
-    field = pltpu.VMEM(current_field.shape, F32)
     operands = (
         current_field, earlier_field, wave_coef, layer_mask, point_owner.reshape(1, points), point_xyz,
         cell_offset.reshape(1, points), wave_vector, frequency.reshape(1, width), amplitude,
@@ -474,21 +485,21 @@
     like = [pltpu.VMEM(a.shape, a.dtype) for a in operands]
     dma = pltpu.SemaphoreType.DMA
     exchanges = 2 * STEPS - 1
-    final_field, prior_field = pl.pallas_call(
-        functools.partial(wave_kernel, (in_row, in_column, in_group)),
-        out_shape=(field, field),
+    held, driven = pl.pallas_call(
+        functools.partial(wave_kernel, (in_x, in_z, in_y, in_group)),
+        out_shape=(
+            pltpu.VMEM((STEPS + 2, 3, nx, ny, nz), F32),
+            pltpu.VMEM((STEPS + 1, 3, nx, ny, nz), F32),
+        ),
         in_specs=[pl.BlockSpec(memory_space=pl.ANY)] * len(operands),
         out_specs=[pl.BlockSpec(memory_space=pltpu.VMEM)] * 2,
         scratch_shapes=[
-            pltpu.VMEM((STEPS + 2, 3, nx, ny, nz), F32),
-            pltpu.VMEM((STEPS + 1, 3, nx, ny, nz), F32),
             like[2], like[3], pltpu.VMEM((nx, ny, nz), F32), *like[4:], dma((len(operands),)),
             pltpu.VMEM((in_group, 8, width), F32), dma((in_group,)), dma((in_group,)),
-            pltpu.VMEM((in_row, in_column, in_group, 1, 4 * SLOTS), F32),
-            pltpu.VMEM((in_row, in_column, in_group, 1, 4 * SLOTS), F32),
-            pltpu.VMEM((in_column, in_row, in_group, 1, 4 * SLOTS), F32),
-            pltpu.VMEM((in_group, in_column, in_row, 1, 4 * SLOTS), F32),
-            dma((3, in_row)), dma((3, in_row)), dma((3,)),
+            pltpu.VMEM((in_y * in_x, in_z * in_group, 1, 4 * SLOTS), F32),
+            pltpu.VMEM((in_y * in_x, in_z * in_group, 1, 4 * SLOTS), F32),
+            pltpu.VMEM((in_z * in_group, in_y * in_x, 1, 4 * SLOTS), F32),
+            dma((2, in_y * in_x)), dma((2, in_y * in_x)), dma((2,)),
             pltpu.VMEM((exchanges, 2, 3, 2, ny, nz), F32),
             pltpu.VMEM((exchanges, 2, 3, nx, 2, nz), F32),
             pltpu.VMEM((exchanges, 2, 3, nx, 2, nz), F32),
@@ -497,10 +508,10 @@
             pltpu.VMEM((modes // 2, width), BF16),
             pltpu.VMEM((modes // 2, width), BF16),
             pltpu.VMEM((2, FIELDS * MODES, modes // 2), F32), dma, dma,
-            pltpu.VMEM((2 * FIELDS * MODES, modes), BF16),
+            pltpu.VMEM((STEPS, 6 * MODES, modes), BF16),
             pltpu.VMEM((3, MODES, slots), F32),
-            pltpu.VMEM((modes, chunk), BF16),
-            pltpu.VMEM((modes, chunk), BF16),
+            pltpu.VMEM((modes, slots), BF16),
+            pltpu.VMEM((modes, slots), BF16),
             pltpu.VMEM((STEPS, 3, slots), F32),
             pltpu.VMEM((nx * ny, slots), BF16),
             pltpu.VMEM((slots, nz), BF16),
@@ -508,10 +519,10 @@
             pltpu.VMEM((3, nx * ny, nz), F32),
         ],
         compiler_params=pltpu.CompilerParams(
-            collective_id=0, has_side_effects=True, vmem_limit_bytes=60400 << 10
+            collective_id=0, has_side_effects=True, vmem_limit_bytes=57600 << 10
         ),
     )(*operands)
-    return final_field, prior_field
+    return held[STEPS + 1] + driven[STEPS], held[STEPS] + driven[STEPS - 1]
 
 
 def solution(mesh):

time: 51.2 us -> 44.5 us (0.87)
  the two profiles are of different devices: /device:TPU:1 before, /device:TPU:0 now
where the time goes in v5:
time: 44.5 us; the launch traced here: 44.3 us
  Pallas kernels  42.7 us (96%)
  other arithmetic  1.01 us (2%)
  between operations  0.64 us (1%)
    pallas_call x1, Pallas kernels, local(): pl.pallas_call(functools.partial(wave_kernel, (in_x, in_z, in_y, in_group...  42.7 us
    add x1, other arithmetic, local(): return (held[STEPS + 1] + driven[STEPS], held[STEPS] + driven[STEPS - 1])  1.01 us

profile of v5, /device:TPU:0, one launch (start us, length us, event | category | flops | bytes accessed | tf_op | source)
XLA Modules:
  0.0 44.3 jit_solution(13774324780571918419)
XLA Ops:
  0.6 42.7 %shard_map.149 = (f32[5,3,8,16,256]{4,3,2,1,0:T(8,128)S(1)}, f32[4,3,8,16,256]{4,3,2,1,0:T(8,128)S(1)}) custom-call(f32[3,8,16,256]{3,2,1,0:T(8,128)} %current_in.1, f32[3,8,16,256]{3,2,1,0:T(8,128)} %earlier_in.1, f32[8,16,256]{2,1,0:T(8,128)} %coef_in.1, s32[8,16,256]{2,1,0:T(8,128)} %mask_in.1, s32[1,1024]{1,0:T(1,128)} %bitcast.9, f32[3,1024]{1,0:T(4,128)} %xyz_in.1, ...), custom_call_target="tpu_custom_call" | custom-call | tf_op jit(solution)/shard_map/pallas_call | solution.py:488
  43.3 1.0 %add_bitcast_fusion = (f32[3,8,16,256]{3,2,1,0:T(8,128)}, f32[3,8,16,256]{3,2,1,0:T(8,128)}) fusion(f32[4,3,8,16,256]{4,3,2,1,0:T(8,128)S(1)} %get-tuple-element.5, f32[5,3,8,16,256]{4,3,2,1,0:T(8,128)S(1)} %get-tuple-element.4), kind=kLoop, calls=%fused_computation | loop fusion | flops 196608 | bytes 2359296 | tf_op jit(solution)/shard_map/add | solution.py:525

commit v6 on v5

--- a/solution.py
+++ b/solution.py
@@ -218,7 +218,7 @@
     split,
     current_in, earlier_in, coef_in, mask_in, owner_in, xyz_in, offset_in, wave_in, freq_in, amp_in, index_in, table_in,
     weight_in, column_in,
-    held, driven,
+    held,
     coef, mask, sign, owner, xyz, offset, wave, freq, amp, index, table, weight, column, load_sem,
     comps, comp_send, comp_recv,
     sent, first, second, hop_send, hop_recv, hop_own,
@@ -250,9 +250,6 @@
     partners = [outer_at(d)[1] for d in range(1, outers)]
     partners += [inner_at(d)[1] for d in range(1, inners)]
     partners += [(after, comp), (before, comp)]
-    for partner in partners:
-        pl.semaphore_signal(barrier, inc=1, device_id=partner, device_id_type=MESH)
-
     loads = [
         pltpu.make_async_copy(a, b, load_sem.at[i])
         for i, (a, b) in enumerate((
@@ -262,7 +259,11 @@
             (coef_in, coef), (earlier_in, held.at[0]), (mask_in, mask),
         ))
     ]
-    for load in loads:
+    for load in loads[:3]:
+        load.start()
+    for partner in partners:
+        pl.semaphore_signal(barrier, inc=1, device_id=partner, device_id_type=MESH)
+    for load in loads[3:]:
         load.start()
     for load in loads[:3]:
         load.wait()
@@ -280,29 +281,32 @@
     comps[0, 7:8, :] = phase
     loads[8].wait()
 
-    def halo_copies(e, u):
+    def halo_copies(e, u, c):
         faces = (
-            (u.at[:, pl.ds(0, 2)], x_in.at[e, 1], (before, comp)),
-            (u.at[:, pl.ds(nx - 2, 2)], x_in.at[e, 0], (after, comp)),
-            (y_out.at[e, 0], y_in.at[e, 1], (slab, left)),
-            (y_out.at[e, 1], y_in.at[e, 0], (slab, right)),
+            (u.at[c, pl.ds(0, 2)], x_in.at[e, 1, c], (before, comp)),
+            (u.at[c, pl.ds(nx - 2, 2)], x_in.at[e, 0, c], (after, comp)),
+            (y_out.at[e, 0, c], y_in.at[e, 1, c], (slab, left)),
+            (y_out.at[e, 1, c], y_in.at[e, 0, c], (slab, right)),
         )
         return [
             pltpu.make_async_remote_copy(
-                src_ref=a, dst_ref=b, send_sem=halo_send.at[e, i], recv_sem=halo_recv.at[e, i],
+                src_ref=a, dst_ref=b, send_sem=halo_send.at[e, c, i], recv_sem=halo_recv.at[e, c, i],
                 device_id=target, device_id_type=MESH,
             )
             for i, (a, b, target) in enumerate(faces)
         ]
 
-    def start_halo(e, u):
-        y_out[e, 0] = u[:, :, 0:2, :]
-        y_out[e, 1] = u[:, :, ny - 2 : ny, :]
-        for copy in halo_copies(e, u):
+    def start_halo(e, u, c):
+        copies = halo_copies(e, u, c)
+        for copy in copies[:2]:
             copy.start()
-
-    def wait_halo(e, u):
-        for copy in halo_copies(e, u):
+        y_out[e, 0, c] = u[c, :, 0:2, :]
+        y_out[e, 1, c] = u[c, :, ny - 2 : ny, :]
+        for copy in copies[2:]:
+            copy.start()
+
+    def wait_halo(e, u, c):
+        for copy in halo_copies(e, u, c):
             copy.wait()
 
     def comp_copy(d):
@@ -337,22 +341,24 @@
     start_hop(0)
     for d in range(1, in_group):
         comp_copy(d).start()
-    start_halo(0, held.at[1])
+    for c in range(3):
+        start_halo(0, held.at[1], c)
     for load in loads[9:]:
         load.wait()
     sign[...] = jnp.where(mask[...] == 1, 1.0, 0.0) - jnp.where(mask[...] == 2, 1.0, 0.0)
 
     lane = lax.broadcasted_iota(jnp.int32, (ny, nz), 1)
 
-    def advance(e, field, i, source):
+    def advance(i, source, send):
         def one(c, carry):
-            low, high = x_in[e, 0, c], x_in[e, 1, c]
+            wait_halo(i, held.at[i + 1], c)
+            low, high = x_in[i, 0, c], x_in[i, 1, c]
             low, high = jnp.where(slab > 0, low, 0.0), jnp.where(slab < slabs - 1, high, 0.0)
-            planes = [low[0], low[1]] + [field[i + 1, c, x] for x in range(nx)] + [high[0], high[1]]
+            planes = [low[0], low[1]] + [held[i + 1, c, x] for x in range(nx)] + [high[0], high[1]]
             for x in range(nx):
                 u = planes[x + 2]
-                back = jnp.where(comp > 0, y_in[e, 0, c, x], 0.0)
-                front = jnp.where(comp < in_group - 1, y_in[e, 1, c, x], 0.0)
+                back = jnp.where(comp > 0, y_in[i, 0, c, x], 0.0)
+                front = jnp.where(comp < in_group - 1, y_in[i, 1, c, x], 0.0)
                 tall = jnp.concatenate([back, u, front], axis=0)
                 near = planes[x + 1] + planes[x + 3]
                 far = planes[x] + planes[x + 4]
@@ -363,10 +369,15 @@
                 far = far + jnp.where(lane >= 2, pltpu.roll(u, 2, 1), 0.0)
                 far = far + jnp.where(lane < nz - 2, pltpu.roll(u, nz - 2, 1), 0.0)
                 curved = centre_weight * u + near_weight * near + far_weight * far
-                following = 2.0 * u - field[i, c, x] + coef[x] * curved
+                following = 2.0 * u - held[i, c, x] + coef[x] * curved
                 if source is not None:
                     following = following + source(c, x)
-                field[i + 2, c, x] = following
+                held[i + 2, c, x] = following
+            if send is not None:
+                @pl.when(send)
+                def _():
+                    start_halo(i + 1, held.at[i + 2], c)
+
             return carry
 
         lax.fori_loop(0, 3, one, 0)
@@ -392,53 +403,52 @@
         return carry
 
     lax.fori_loop(0, in_group, one_block, 0)
-    half_copy = pltpu.make_async_remote_copy(
-        src_ref=f_ref.at[core], dst_ref=f_ref.at[core], send_sem=f_send, recv_sem=f_recv,
-        device_id=(slab, comp + 1 - 2 * core), device_id_type=MESH,
-    )
-    half_copy.start()
-    wait_halo(0, held.at[1])
-    advance(0, held, 0, None)
-    start_halo(1, held.at[2])
+    half_copies = [
+        pltpu.make_async_remote_copy(
+            src_ref=f_ref.at[core, pl.ds(n * 3 * MODES, 3 * MODES)],
+            dst_ref=f_ref.at[core, pl.ds(n * 3 * MODES, 3 * MODES)],
+            send_sem=f_send.at[n], recv_sem=f_recv.at[n],
+            device_id=(slab, comp + 1 - 2 * core), device_id_type=MESH,
+        )
+        for n in range(STEPS)
+    ]
+    for copy in half_copies:
+        copy.start()
+    advance(0, None, None)
     wait_hop(1)
     arrived = second[...].reshape(slabs * in_group, 4 * SLOTS)
     px, py, pz, cell = slot_rows(arrived)
     point_modes([px, py, pz], t_ref)
     hot_rows(arrived, cell, xy_hot, z_hot)
-    chunk = 256
-
-    def lanes_of(i):
+    def lanes_of(i, chunk):
         return pl.ds(pl.multiple_of(i * chunk, chunk), chunk)
 
     def one_product(i, carry):
-        point_products(t_ref, lanes_of(i), w_hi, w_lo)
+        point_products(t_ref, lanes_of(i, narrow), w_hi, w_lo)
         return carry
 
-    chunks = t_ref.shape[2] // chunk
-    lax.fori_loop(0, chunks, one_product, 0)
-    half_copy.wait()
+    slots = t_ref.shape[2]
+    narrow, broad = min(slots, 256), min(slots, 1024)
+    lax.fori_loop(0, slots // narrow, one_product, 0)
     rows = 3 * MODES
-    for which in (0, 1):
-        lanes = pl.ds(which * wide, wide)
-        for n in range(STEPS):
+
+    def take_half(n):
+        half_copies[n].wait()
+        for which in (0, 1):
+            lanes = pl.ds(which * wide, wide)
             f[n, :rows, lanes], f[n, rows:, lanes] = split2(f_ref[which, n * rows : (n + 1) * rows, :])
-    driven[0] = jnp.zeros_like(driven[0])
 
     def one_step(n, carry):
-        @pl.when(n > 0)
-        def _():
-            wait_halo(n, held.at[n + 1])
-            advance(n, held, n, None)
-
-        @pl.when((n > 0) & (n < STEPS - 1))
-        def _():
-            start_halo(n + 1, held.at[n + 2])
+        for step in range(STEPS):
+            @pl.when(n == step)
+            def _(step=step):
+                take_half(step)
 
         def one_chunk(i, inner):
-            point_sums(n, t_ref, lanes_of(i), f, w_hi, w_lo, v_ref)
+            point_sums(n, t_ref, lanes_of(i, broad), f, w_hi, w_lo, v_ref)
             return inner
 
-        lax.fori_loop(0, chunks, one_chunk, 0)
+        lax.fori_loop(0, slots // broad, one_chunk, 0)
         spread_fields(v_ref[n], xy_hot, z_hot, spread, forcing)
 
         def source(c, x):
@@ -448,19 +458,15 @@
         def _():
             def one(c, inner):
                 for x in range(nx):
-                    driven[1, c, x] = source(c, x)
+                    held[2, c, x] += source(c, x)
+                start_halo(1, held.at[2], c)
                 return inner
 
             lax.fori_loop(0, 3, one, 0)
 
         @pl.when(n > 0)
         def _():
-            wait_halo(STEPS + n - 1, driven.at[n])
-            advance(STEPS + n - 1, driven, n - 1, source)
-
-        @pl.when(n < STEPS - 1)
-        def _():
-            start_halo(STEPS + n, driven.at[n + 1])
+            advance(n, source, n < STEPS - 1)
 
         return carry
 
@@ -484,15 +490,12 @@
     )
     like = [pltpu.VMEM(a.shape, a.dtype) for a in operands]
     dma = pltpu.SemaphoreType.DMA
-    exchanges = 2 * STEPS - 1
-    held, driven = pl.pallas_call(
+    exchanges = STEPS
+    held = pl.pallas_call(
         functools.partial(wave_kernel, (in_x, in_z, in_y, in_group)),
-        out_shape=(
-            pltpu.VMEM((STEPS + 2, 3, nx, ny, nz), F32),
-            pltpu.VMEM((STEPS + 1, 3, nx, ny, nz), F32),
-        ),
+        out_shape=pltpu.VMEM((STEPS + 2, 3, nx, ny, nz), F32),
         in_specs=[pl.BlockSpec(memory_space=pl.ANY)] * len(operands),
-        out_specs=[pl.BlockSpec(memory_space=pltpu.VMEM)] * 2,
+        out_specs=pl.BlockSpec(memory_space=pltpu.VMEM),
         scratch_shapes=[
             like[2], like[3], pltpu.VMEM((nx, ny, nz), F32), *like[4:], dma((len(operands),)),
             pltpu.VMEM((in_group, 8, width), F32), dma((in_group,)), dma((in_group,)),
@@ -503,11 +506,11 @@
             pltpu.VMEM((exchanges, 2, 3, 2, ny, nz), F32),
             pltpu.VMEM((exchanges, 2, 3, nx, 2, nz), F32),
             pltpu.VMEM((exchanges, 2, 3, nx, 2, nz), F32),
-            dma((exchanges, 4)), dma((exchanges, 4)),
+            dma((exchanges, 3, 4)), dma((exchanges, 3, 4)),
             pltpu.VMEM((2 * FIELDS * MODES, width), BF16),
             pltpu.VMEM((modes // 2, width), BF16),
             pltpu.VMEM((modes // 2, width), BF16),
-            pltpu.VMEM((2, FIELDS * MODES, modes // 2), F32), dma, dma,
+            pltpu.VMEM((2, FIELDS * MODES, modes // 2), F32), dma((STEPS,)), dma((STEPS,)),
             pltpu.VMEM((STEPS, 6 * MODES, modes), BF16),
             pltpu.VMEM((3, MODES, slots), F32),
             pltpu.VMEM((modes, slots), BF16),
@@ -519,10 +522,10 @@
             pltpu.VMEM((3, nx * ny, nz), F32),
         ],
         compiler_params=pltpu.CompilerParams(
-            collective_id=0, has_side_effects=True, vmem_limit_bytes=57600 << 10
+            collective_id=0, has_side_effects=True, vmem_limit_bytes=59200 << 10
         ),
     )(*operands)
-    return held[STEPS + 1] + driven[STEPS], held[STEPS] + driven[STEPS - 1]
+    return held[STEPS + 1], held[STEPS]
 
 
 def solution(mesh):

time: 44.5 us -> 41.3 us (0.928)
  Pallas kernels: 42.7 us -> 39.6 us
  other arithmetic: 1.01 us -> 0 us
  local copies, waits for them, and re-layouts: 0 us -> 0.96 us
    pallas_call x1, Pallas kernels: 42.7 us -> 39.6 us  [local(): pl.pallas_call(functools.partial(wave_kernel, (in_x, in_z, in_y, in_group...]
    add x1 -> x0, other arithmetic: 1.01 us -> none  [local(): return (held[STEPS + 1] + driven[STEPS], held[STEPS] + driven[STEPS - 1])]
    squeeze x0 -> x1, local copies, waits for them, and re-layouts: none -> 0.96 us  [local(): return (held[STEPS + 1], held[STEPS])]
where the time goes in v6:
time: 41.3 us; the launch traced here: 41.2 us
  Pallas kernels  39.6 us (96%)
  local copies, waits for them, and re-layouts  0.96 us (2%)
  between operations  0.64 us (2%)
    pallas_call x1, Pallas kernels, local(): pl.pallas_call(functools.partial(wave_kernel, (in_x, in_z, in_y, in_group...  39.6 us
    squeeze x1, local copies, waits for them, and re-layouts, local(): return (held[STEPS + 1], held[STEPS])  0.96 us

profile of v6, /device:TPU:0, one launch (start us, length us, event | category | flops | bytes accessed | tf_op | source)
XLA Modules:
  0.0 41.2 jit_solution(14417694300172647176)
XLA Ops:
  0.6 39.6 %shard_map.149 = f32[5,3,8,16,256]{4,3,2,1,0:T(8,128)S(1)} custom-call(f32[3,8,16,256]{3,2,1,0:T(8,128)} %current_in.1, f32[3,8,16,256]{3,2,1,0:T(8,128)} %earlier_in.1, f32[8,16,256]{2,1,0:T(8,128)} %coef_in.1, s32[8,16,256]{2,1,0:T(8,128)} %mask_in.1, s32[1,1024]{1,0:T(1,128)} %bitcast.9, f32[3,1024]{1,0:T(4,128)} %xyz_in.1, s32[1,1024]{1,0:T(1,128)} %bitcast.10, ...), custom_call_target="tpu_custom_call" | custom-call | tf_op jit(solution)/shard_map/pallas_call | solution.py:494
  40.2 1.0 %slice_bitcast_fusion = (f32[3,8,16,256]{3,2,1,0:T(8,128)}, f32[3,8,16,256]{3,2,1,0:T(8,128)}) fusion(f32[5,3,8,16,256]{4,3,2,1,0:T(8,128)S(1)} %shard_map.149), kind=kLoop, calls=%fused_computation | loop fusion | bytes 1572864 | tf_op jit(solution)/shard_map/squeeze | solution.py:528

commit v7 on v6

--- a/solution.py
+++ b/solution.py
@@ -155,18 +155,19 @@
         v_ref[n, i : i + 1, lanes] = jnp.sum(sums[i * MODES : (i + 1) * MODES, :] * tz, axis=0, keepdims=True)
 
 
-def hot_rows(arrived, cell, xy_hot, z_hot):
-    depth = z_hot.shape[1]
+def hot_rows(cell, xy_hot, depth):
     place = jnp.floor((cell - 1.0) * (1.0 / depth))
     xy_hot[...] = jnp.where(
         place == lax.broadcasted_iota(jnp.int32, xy_hot.shape, 0).astype(F32), 1.0, 0.0
     ).astype(BF16)
-    sources = arrived.shape[0]
+
+
+def hot_columns(along, first, last, z_hot):
+    depth = z_hot.shape[1]
+    sources = along.shape[0]
     lane = lax.broadcasted_iota(jnp.int32, (sources, depth), 1).astype(F32)
-    for r in range(SLOTS):
-        one = arrived[:, 3 * SLOTS + r : 3 * SLOTS + r + 1] - 1.0
-        along = one - jnp.floor(one * (1.0 / depth)) * depth
-        z_hot[r * sources : (r + 1) * sources, :] = jnp.where(along == lane, 1.0, 0.0).astype(BF16)
+    for r in range(first, last):
+        z_hot[r * sources : (r + 1) * sources, :] = jnp.where(along[:, r : r + 1] == lane, 1.0, 0.0).astype(BF16)
 
 
 def spread_fields(v, xy_hot, z_hot, spread, forcing):
@@ -419,17 +420,14 @@
     arrived = second[...].reshape(slabs * in_group, 4 * SLOTS)
     px, py, pz, cell = slot_rows(arrived)
     point_modes([px, py, pz], t_ref)
-    hot_rows(arrived, cell, xy_hot, z_hot)
+    cells = arrived[:, 3 * SLOTS :] - 1.0
+    along = cells - jnp.floor(cells * (1.0 / nz)) * nz
     def lanes_of(i, chunk):
         return pl.ds(pl.multiple_of(i * chunk, chunk), chunk)
 
-    def one_product(i, carry):
-        point_products(t_ref, lanes_of(i, narrow), w_hi, w_lo)
-        return carry
-
     slots = t_ref.shape[2]
-    narrow, broad = min(slots, 256), min(slots, 1024)
-    lax.fori_loop(0, slots // narrow, one_product, 0)
+    narrow, broad = slots // 4, min(slots, 1024)
+    point_products(t_ref, pl.ds(0, narrow), w_hi, w_lo)
     rows = 3 * MODES
 
     def take_half(n):
@@ -438,8 +436,30 @@
             lanes = pl.ds(which * wide, wide)
             f[n, :rows, lanes], f[n, rows:, lanes] = split2(f_ref[which, n * rows : (n + 1) * rows, :])
 
+    take_half(0)
+    for i in range(4):
+        point_sums(0, t_ref, pl.ds(i * narrow, narrow), f, w_hi, w_lo, v_ref)
+        if i < 3:
+            point_products(t_ref, pl.ds((i + 1) * narrow, narrow), w_hi, w_lo)
+            hot_columns(along, i * SLOTS // 4, (i + 1) * SLOTS // 4, z_hot)
+        else:
+            hot_columns(along, i * SLOTS // 4, SLOTS, z_hot)
+            hot_rows(cell, xy_hot, nz)
+    spread_fields(v_ref[0], xy_hot, z_hot, spread, forcing)
+
+    def source(c, x):
+        return sign[x] * forcing[c, x * ny : (x + 1) * ny, :]
+
+    def first_step(c, carry):
+        for x in range(nx):
+            held[2, c, x] += source(c, x)
+        start_halo(1, held.at[2], c)
+        return carry
+
+    lax.fori_loop(0, 3, first_step, 0)
+
     def one_step(n, carry):
-        for step in range(STEPS):
+        for step in range(1, STEPS):
             @pl.when(n == step)
             def _(step=step):
                 take_half(step)
@@ -451,26 +471,10 @@
         lax.fori_loop(0, slots // broad, one_chunk, 0)
         spread_fields(v_ref[n], xy_hot, z_hot, spread, forcing)
 
-        def source(c, x):
-            return sign[x] * forcing[c, x * ny : (x + 1) * ny, :]
-
-        @pl.when(n == 0)
-        def _():
-            def one(c, inner):
-                for x in range(nx):
-                    held[2, c, x] += source(c, x)
-                start_halo(1, held.at[2], c)
-                return inner
-
-            lax.fori_loop(0, 3, one, 0)
-
-        @pl.when(n > 0)
-        def _():
-            advance(n, source, n < STEPS - 1)
-
+        advance(n, source, n < STEPS - 1)
         return carry
 
-    lax.fori_loop(0, STEPS, one_step, 0)
+    lax.fori_loop(1, STEPS, one_step, 0)
 
 def local(current_field, earlier_field, wave_coef, layer_mask, point_xyz, point_owner, cell_offset, wave_vector, frequency, amplitude, phase_index, phase_table):
     slabs, in_group = lax.axis_size("slab"), lax.axis_size("comp")

time: 41.3 us -> 39.2 us (0.949)
  Pallas kernels: 39.6 us -> 37.5 us
    pallas_call x1, Pallas kernels: 39.6 us -> 37.5 us  [local(): pl.pallas_call(functools.partial(wave_kernel, (in_x, in_z, in_y, in_group...]
where the time goes in v7:
time: 39.2 us; the launch traced here: 39.1 us
  Pallas kernels  37.5 us (96%)
  local copies, waits for them, and re-layouts  0.96 us (2%)
  between operations  0.64 us (2%)
    pallas_call x1, Pallas kernels, local(): pl.pallas_call(functools.partial(wave_kernel, (in_x, in_z, in_y, in_group...  37.5 us
    squeeze x1, local copies, waits for them, and re-layouts, local(): return (held[STEPS + 1], held[STEPS])  0.96 us

profile of v7, /device:TPU:0, one launch (start us, length us, event | category | flops | bytes accessed | tf_op | source)
XLA Modules:
  0.0 39.1 jit_solution(18402023049182957033)
XLA Ops:
  0.6 37.5 %shard_map.149 = f32[5,3,8,16,256]{4,3,2,1,0:T(8,128)S(1)} custom-call(f32[3,8,16,256]{3,2,1,0:T(8,128)} %current_in.1, f32[3,8,16,256]{3,2,1,0:T(8,128)} %earlier_in.1, f32[8,16,256]{2,1,0:T(8,128)} %coef_in.1, s32[8,16,256]{2,1,0:T(8,128)} %mask_in.1, s32[1,1024]{1,0:T(1,128)} %bitcast.9, f32[3,1024]{1,0:T(4,128)} %xyz_in.1, s32[1,1024]{1,0:T(1,128)} %bitcast.10, ...), custom_call_target="tpu_custom_call" | custom-call | tf_op jit(solution)/shard_map/pallas_call | solution.py:498
  38.1 1.0 %slice_bitcast_fusion = (f32[3,8,16,256]{3,2,1,0:T(8,128)}, f32[3,8,16,256]{3,2,1,0:T(8,128)}) fusion(f32[5,3,8,16,256]{4,3,2,1,0:T(8,128)S(1)} %shard_map.149), kind=kLoop, calls=%fused_computation | loop fusion | bytes 1572864 | tf_op jit(solution)/shard_map/squeeze | solution.py:532

commit v8 on v7

--- a/solution.py
+++ b/solution.py
@@ -245,7 +245,7 @@
         return there, ((y * in_z + there // in_group) * in_x + x, there % in_group)
 
     def group_at(d):
-        return lax.rem(comp + d, in_group)
+        return comp + lax.rem(d, 2) * (1 - 2 * lax.rem(comp, 2)) + (d // 2) * (2 - 4 * (comp // 2))
 
     barrier = pltpu.get_barrier_semaphore()
     partners = [outer_at(d)[1] for d in range(1, outers)]
@@ -297,14 +297,19 @@
             for i, (a, b, target) in enumerate(faces)
         ]
 
-    def start_halo(e, u, c):
-        copies = halo_copies(e, u, c)
-        for copy in copies[:2]:
+    def start_x(e, u, c):
+        for copy in halo_copies(e, u, c)[:2]:
             copy.start()
+
+    def start_y(e, u, c):
         y_out[e, 0, c] = u[c, :, 0:2, :]
         y_out[e, 1, c] = u[c, :, ny - 2 : ny, :]
-        for copy in copies[2:]:
+        for copy in halo_copies(e, u, c)[2:]:
             copy.start()
+
+    def start_halo(e, u, c):
+        start_x(e, u, c)
+        start_y(e, u, c)
 
     def wait_halo(e, u, c):
         for copy in halo_copies(e, u, c):
@@ -349,6 +354,8 @@
     sign[...] = jnp.where(mask[...] == 1, 1.0, 0.0) - jnp.where(mask[...] == 2, 1.0, 0.0)
 
     lane = lax.broadcasted_iota(jnp.int32, (ny, nz), 1)
+    outside = [0, 1, nx - 2, nx - 1]
+    inside = list(range(2, nx - 2))
 
     def advance(i, source, send):
         def one(c, carry):
@@ -356,7 +363,12 @@
             low, high = x_in[i, 0, c], x_in[i, 1, c]
             low, high = jnp.where(slab > 0, low, 0.0), jnp.where(slab < slabs - 1, high, 0.0)
             planes = [low[0], low[1]] + [held[i + 1, c, x] for x in range(nx)] + [high[0], high[1]]
-            for x in range(nx):
+            for x in outside + inside:
+                if x == inside[0] and send is not None:
+                    @pl.when(send)
+                    def _():
+                        start_x(i + 1, held.at[i + 2], c)
+
                 u = planes[x + 2]
                 back = jnp.where(comp > 0, y_in[i, 0, c, x], 0.0)
                 front = jnp.where(comp < in_group - 1, y_in[i, 1, c, x], 0.0)
@@ -377,7 +389,7 @@
             if send is not None:
                 @pl.when(send)
                 def _():
-                    start_halo(i + 1, held.at[i + 2], c)
+                    start_y(i + 1, held.at[i + 2], c)
 
             return carry
 
@@ -396,7 +408,7 @@
         mode_sums(comps[i], weight[...], column[...], odd, q, p_hi, p_lo)
         f_ref[core] += mode_products(q, p_hi, p_lo)
 
-        @pl.when(i == 1)
+        @pl.when(i == 2)
         def _():
             wait_hop(0)
             start_hop(1)
@@ -450,13 +462,20 @@
     def source(c, x):
         return sign[x] * forcing[c, x * ny : (x + 1) * ny, :]
 
-    def first_step(c, carry):
-        for x in range(nx):
+    def first_outside(c, carry):
+        for x in outside:
             held[2, c, x] += source(c, x)
-        start_halo(1, held.at[2], c)
+        start_x(1, held.at[2], c)
         return carry
 
-    lax.fori_loop(0, 3, first_step, 0)
+    def first_inside(c, carry):
+        for x in inside:
+            held[2, c, x] += source(c, x)
+        start_y(1, held.at[2], c)
+        return carry
+
+    lax.fori_loop(0, 3, first_outside, 0)
+    lax.fori_loop(0, 3, first_inside, 0)
 
     def one_step(n, carry):
         for step in range(1, STEPS):

time: 39.2 us -> 38.7 us (0.987)
  Pallas kernels: 37.5 us -> 36.9 us
    pallas_call x1, Pallas kernels: 37.5 us -> 36.9 us  [local(): pl.pallas_call(functools.partial(wave_kernel, (in_x, in_z, in_y, in_group...]
where the time goes in v8:
time: 38.7 us; the launch traced here: 38.5 us
  Pallas kernels  36.9 us (95%)
  local copies, waits for them, and re-layouts  0.96 us (2%)
  between operations  0.64 us (2%)
    pallas_call x1, Pallas kernels, local(): pl.pallas_call(functools.partial(wave_kernel, (in_x, in_z, in_y, in_group...  36.9 us
    squeeze x1, local copies, waits for them, and re-layouts, local(): return (held[STEPS + 1], held[STEPS])  0.96 us

profile of v8, /device:TPU:0, one launch (start us, length us, event | category | flops | bytes accessed | tf_op | source)
XLA Modules:
  0.0 38.5 jit_solution(14014098586052841021)
XLA Ops:
  0.6 36.9 %shard_map.149 = f32[5,3,8,16,256]{4,3,2,1,0:T(8,128)S(1)} custom-call(f32[3,8,16,256]{3,2,1,0:T(8,128)} %current_in.1, f32[3,8,16,256]{3,2,1,0:T(8,128)} %earlier_in.1, f32[8,16,256]{2,1,0:T(8,128)} %coef_in.1, s32[8,16,256]{2,1,0:T(8,128)} %mask_in.1, s32[1,1024]{1,0:T(1,128)} %bitcast.9, f32[3,1024]{1,0:T(4,128)} %xyz_in.1, s32[1,1024]{1,0:T(1,128)} %bitcast.10, ...), custom_call_target="tpu_custom_call" | custom-call | tf_op jit(solution)/shard_map/pallas_call | solution.py:517
  37.5 1.0 %slice_bitcast_fusion = (f32[3,8,16,256]{3,2,1,0:T(8,128)}, f32[3,8,16,256]{3,2,1,0:T(8,128)}) fusion(f32[5,3,8,16,256]{4,3,2,1,0:T(8,128)S(1)} %shard_map.149), kind=kLoop, calls=%fused_computation | loop fusion | bytes 1572864 | tf_op jit(solution)/shard_map/squeeze | solution.py:551

commit v9 on v8

--- a/solution.py
+++ b/solution.py
@@ -224,6 +224,7 @@
     comps, comp_send, comp_recv,
     sent, first, second, hop_send, hop_recv, hop_own,
     x_in, y_in, y_out, halo_send, halo_recv,
+    far_in, corner_in, wide_send, wide_recv, push_in, push_out, coef_far, flat_send, flat_recv,
     q, p_hi, p_lo, f_ref, f_send, f_recv, f, t_ref, w_hi, w_lo, v_ref, xy_hot, z_hot, spread, forcing,
 ):
     in_x, in_z, in_y, in_group = split
@@ -250,7 +251,7 @@
     barrier = pltpu.get_barrier_semaphore()
     partners = [outer_at(d)[1] for d in range(1, outers)]
     partners += [inner_at(d)[1] for d in range(1, inners)]
-    partners += [(after, comp), (before, comp)]
+    partners += [(a, c) for a in (after, before) for c in (comp, left, right)]
     loads = [
         pltpu.make_async_copy(a, b, load_sem.at[i])
         for i, (a, b) in enumerate((
@@ -311,9 +312,46 @@
         start_x(e, u, c)
         start_y(e, u, c)
 
-    def wait_halo(e, u, c):
-        for copy in halo_copies(e, u, c):
+    def wait_halo(e, u, c, faces):
+        for copy in halo_copies(e, u, c)[faces]:
             copy.wait()
+
+    def wide_copies(c):
+        u, edge = held.at[2], y_out.at[1]
+        moves = (
+            (u.at[c, pl.ds(2, 2)], far_in.at[1, c], (before, comp)),
+            (u.at[c, pl.ds(nx - 4, 2)], far_in.at[0, c], (after, comp)),
+            (edge.at[0, c, pl.ds(0, 2)], corner_in.at[1, 1, c], (before, left)),
+            (edge.at[1, c, pl.ds(0, 2)], corner_in.at[1, 0, c], (before, right)),
+            (edge.at[0, c, pl.ds(nx - 2, 2)], corner_in.at[0, 1, c], (after, left)),
+            (edge.at[1, c, pl.ds(nx - 2, 2)], corner_in.at[0, 0, c], (after, right)),
+        )
+        return [
+            pltpu.make_async_remote_copy(
+                src_ref=a, dst_ref=b, send_sem=wide_send.at[c, i], recv_sem=wide_recv.at[c, i],
+                device_id=target, device_id_type=MESH,
+            )
+            for i, (a, b, target) in enumerate(moves)
+        ]
+
+    def flat_copies(kind):
+        if kind == 0:
+            moves = (
+                (coef.at[pl.ds(0, 2)], coef_far.at[1], (before, comp)),
+                (coef.at[pl.ds(nx - 2, 2)], coef_far.at[0], (after, comp)),
+            )
+        else:
+            moves = (
+                (push_out.at[0], push_in.at[1], (before, comp)),
+                (push_out.at[1], push_in.at[0], (after, comp)),
+            )
+        return [
+            pltpu.make_async_remote_copy(
+                src_ref=a, dst_ref=b, send_sem=flat_send.at[kind, i], recv_sem=flat_recv.at[kind, i],
+                device_id=target, device_id_type=MESH,
+            )
+            for i, (a, b, target) in enumerate(moves)
+        ]
 
     def comp_copy(d):
         return pltpu.make_async_remote_copy(
@@ -351,49 +389,58 @@
         start_halo(0, held.at[1], c)
     for load in loads[9:]:
         load.wait()
+    for copy in flat_copies(0):
+        copy.start()
     sign[...] = jnp.where(mask[...] == 1, 1.0, 0.0) - jnp.where(mask[...] == 2, 1.0, 0.0)
 
     lane = lax.broadcasted_iota(jnp.int32, (ny, nz), 1)
     outside = [0, 1, nx - 2, nx - 1]
     inside = list(range(2, nx - 2))
 
-    def advance(i, source, send):
+    def curve(row, back, front):
+        u = row[2]
+        tall = jnp.concatenate([jnp.where(comp > 0, back, 0.0), u, jnp.where(comp < in_group - 1, front, 0.0)], axis=0)
+        near = row[1] + row[3]
+        far = row[0] + row[4]
+        near = near + (tall[1 : ny + 1] + tall[3 : ny + 3])
+        far = far + (tall[0:ny] + tall[4 : ny + 4])
+        near = near + jnp.where(lane >= 1, pltpu.roll(u, 1, 1), 0.0)
+        near = near + jnp.where(lane < nz - 1, pltpu.roll(u, nz - 1, 1), 0.0)
+        far = far + jnp.where(lane >= 2, pltpu.roll(u, 2, 1), 0.0)
+        far = far + jnp.where(lane < nz - 2, pltpu.roll(u, nz - 2, 1), 0.0)
+        return centre_weight * u + near_weight * near + far_weight * far
+
+    def advance(i, source, faces, send):
         def one(c, carry):
-            wait_halo(i, held.at[i + 1], c)
+            wait_halo(i, held.at[i + 1], c, faces)
             low, high = x_in[i, 0, c], x_in[i, 1, c]
             low, high = jnp.where(slab > 0, low, 0.0), jnp.where(slab < slabs - 1, high, 0.0)
             planes = [low[0], low[1]] + [held[i + 1, c, x] for x in range(nx)] + [high[0], high[1]]
-            for x in outside + inside:
-                if x == inside[0] and send is not None:
-                    @pl.when(send)
-                    def _():
-                        start_x(i + 1, held.at[i + 2], c)
-
-                u = planes[x + 2]
-                back = jnp.where(comp > 0, y_in[i, 0, c, x], 0.0)
-                front = jnp.where(comp < in_group - 1, y_in[i, 1, c, x], 0.0)
-                tall = jnp.concatenate([back, u, front], axis=0)
-                near = planes[x + 1] + planes[x + 3]
-                far = planes[x] + planes[x + 4]
-                near = near + (tall[1 : ny + 1] + tall[3 : ny + 3])
-                far = far + (tall[0:ny] + tall[4 : ny + 4])
-                near = near + jnp.where(lane >= 1, pltpu.roll(u, 1, 1), 0.0)
-                near = near + jnp.where(lane < nz - 1, pltpu.roll(u, nz - 1, 1), 0.0)
-                far = far + jnp.where(lane >= 2, pltpu.roll(u, 2, 1), 0.0)
-                far = far + jnp.where(lane < nz - 2, pltpu.roll(u, nz - 2, 1), 0.0)
-                curved = centre_weight * u + near_weight * near + far_weight * far
-                following = 2.0 * u - held[i, c, x] + coef[x] * curved
+            for x in range(nx):
+                curved = curve(planes[x : x + 5], y_in[i, 0, c, x], y_in[i, 1, c, x])
+                following = 2.0 * planes[x + 2] - held[i, c, x] + coef[x] * curved
                 if source is not None:
                     following = following + source(c, x)
                 held[i + 2, c, x] = following
-            if send is not None:
-                @pl.when(send)
-                def _():
-                    start_y(i + 1, held.at[i + 2], c)
-
+            if send:
+                start_y(i + 1, held.at[i + 2], c)
             return carry
 
         lax.fori_loop(0, 3, one, 0)
+
+    def advance_outside(c, carry):
+        for copy in wide_copies(c):
+            copy.wait()
+        near, own = [x_in[1, side, c] for side in (0, 1)], held.at[2, c]
+        low = [far_in[0, c, 0], far_in[0, c, 1], near[0][0], near[0][1], own[0], own[1]]
+        high = [own[nx - 2], own[nx - 1], near[1][0], near[1][1], far_in[1, c, 0], far_in[1, c, 1]]
+        for side, row in enumerate((low, high)):
+            for k in (0, 1):
+                curved = curve(row[k : k + 5], corner_in[side, 0, c, k], corner_in[side, 1, c, k])
+                x_in[2, side, c, k] = (
+                    2.0 * row[k + 2] - x_in[0, side, c, k] + coef_far[side, k] * curved + push_in[side, c, k]
+                )
+        return carry
 
     wide = 2 * HALF * HALF
     core = lax.rem(comp, 2)
@@ -427,7 +474,7 @@
     ]
     for copy in half_copies:
         copy.start()
-    advance(0, None, None)
+    advance(0, None, slice(0, 4), False)
     wait_hop(1)
     arrived = second[...].reshape(slabs * in_group, 4 * SLOTS)
     px, py, pz, cell = slot_rows(arrived)
@@ -472,28 +519,42 @@
         for x in inside:
             held[2, c, x] += source(c, x)
         start_y(1, held.at[2], c)
+        for copy in wide_copies(c):
+            copy.start()
         return carry
 
     lax.fori_loop(0, 3, first_outside, 0)
     lax.fori_loop(0, 3, first_inside, 0)
 
-    def one_step(n, carry):
-        for step in range(1, STEPS):
-            @pl.when(n == step)
-            def _(step=step):
-                take_half(step)
-
-        def one_chunk(i, inner):
+    def next_forcing(n):
+        take_half(n)
+
+        def one_chunk(i, carry):
             point_sums(n, t_ref, lanes_of(i, broad), f, w_hi, w_lo, v_ref)
-            return inner
+            return carry
 
         lax.fori_loop(0, slots // broad, one_chunk, 0)
         spread_fields(v_ref[n], xy_hot, z_hot, spread, forcing)
 
-        advance(n, source, n < STEPS - 1)
+    next_forcing(1)
+
+    def push(c, carry):
+        for side, first_plane in enumerate((0, nx - 2)):
+            for k in (0, 1):
+                push_out[side, c, k] = source(c, first_plane + k)
         return carry
 
-    lax.fori_loop(1, STEPS, one_step, 0)
+    lax.fori_loop(0, 3, push, 0)
+    for copy in flat_copies(1):
+        copy.start()
+    advance(1, source, slice(0, 4), True)
+    next_forcing(2)
+    for kind in (0, 1):
+        for copy in flat_copies(kind):
+            copy.wait()
+    lax.fori_loop(0, 3, advance_outside, 0)
+    advance(2, source, slice(2, 4), False)
+
 
 def local(current_field, earlier_field, wave_coef, layer_mask, point_xyz, point_owner, cell_offset, wave_vector, frequency, amplitude, phase_index, phase_table):
     slabs, in_group = lax.axis_size("slab"), lax.axis_size("comp")
@@ -530,6 +591,9 @@
             pltpu.VMEM((exchanges, 2, 3, nx, 2, nz), F32),
             pltpu.VMEM((exchanges, 2, 3, nx, 2, nz), F32),
             dma((exchanges, 3, 4)), dma((exchanges, 3, 4)),
+            pltpu.VMEM((2, 3, 2, ny, nz), F32), pltpu.VMEM((2, 2, 3, 2, 2, nz), F32), dma((3, 6)), dma((3, 6)),
+            pltpu.VMEM((2, 3, 2, ny, nz), F32), pltpu.VMEM((2, 3, 2, ny, nz), F32), pltpu.VMEM((2, 2, ny, nz), F32),
+            dma((2, 2)), dma((2, 2)),
             pltpu.VMEM((2 * FIELDS * MODES, width), BF16),
             pltpu.VMEM((modes // 2, width), BF16),
             pltpu.VMEM((modes // 2, width), BF16),

time: 38.7 us -> 41.4 us (1.070)
  the two profiles are of different devices: /device:TPU:0 before, /device:TPU:1 now
where the time goes in v9:
time: 41.4 us; the launch traced here: 41.3 us
  Pallas kernels  39.7 us (96%)
  local copies, waits for them, and re-layouts  0.96 us (2%)
  between operations  0.64 us (2%)
    pallas_call x1, Pallas kernels, local(): pl.pallas_call(functools.partial(wave_kernel, (in_x, in_z, in_y, in_group...  39.7 us
    squeeze x1, local copies, waits for them, and re-layouts, local(): return (held[STEPS + 1], held[STEPS])  0.96 us

profile of v9, /device:TPU:1, one launch (start us, length us, event | category | flops | bytes accessed | tf_op | source)
XLA Modules:
  0.0 41.3 jit_solution(1894286716624899573)
XLA Ops:
  0.6 39.7 %shard_map.149 = f32[5,3,8,16,256]{4,3,2,1,0:T(8,128)S(1)} custom-call(f32[3,8,16,256]{3,2,1,0:T(8,128)} %current_in.1, f32[3,8,16,256]{3,2,1,0:T(8,128)} %earlier_in.1, f32[8,16,256]{2,1,0:T(8,128)} %coef_in.1, s32[8,16,256]{2,1,0:T(8,128)} %mask_in.1, s32[1,1024]{1,0:T(1,128)} %bitcast.9, f32[3,1024]{1,0:T(4,128)} %xyz_in.1, s32[1,1024]{1,0:T(1,128)} %bitcast.10, ...), custom_call_target="tpu_custom_call" | custom-call | tf_op jit(solution)/shard_map/pallas_call | solution.py:578
  40.3 1.0 %slice_bitcast_fusion = (f32[3,8,16,256]{3,2,1,0:T(8,128)}, f32[3,8,16,256]{3,2,1,0:T(8,128)}) fusion(f32[5,3,8,16,256]{4,3,2,1,0:T(8,128)S(1)} %shard_map.149), kind=kLoop, calls=%fused_computation | loop fusion | bytes 1572864 | tf_op jit(solution)/shard_map/squeeze | solution.py:615

commit v10 on v8

--- a/solution.py
+++ b/solution.py
@@ -311,8 +311,8 @@
         start_x(e, u, c)
         start_y(e, u, c)
 
-    def wait_halo(e, u, c):
-        for copy in halo_copies(e, u, c):
+    def wait_halo(e, u, c, faces):
+        for copy in halo_copies(e, u, c)[faces]:
             copy.wait()
 
     def comp_copy(d):
@@ -358,17 +358,8 @@
     inside = list(range(2, nx - 2))
 
     def advance(i, source, send):
-        def one(c, carry):
-            wait_halo(i, held.at[i + 1], c)
-            low, high = x_in[i, 0, c], x_in[i, 1, c]
-            low, high = jnp.where(slab > 0, low, 0.0), jnp.where(slab < slabs - 1, high, 0.0)
-            planes = [low[0], low[1]] + [held[i + 1, c, x] for x in range(nx)] + [high[0], high[1]]
-            for x in outside + inside:
-                if x == inside[0] and send is not None:
-                    @pl.when(send)
-                    def _():
-                        start_x(i + 1, held.at[i + 2], c)
-
+        def some(c, planes, which):
+            for x in which:
                 u = planes[x + 2]
                 back = jnp.where(comp > 0, y_in[i, 0, c, x], 0.0)
                 front = jnp.where(comp < in_group - 1, y_in[i, 1, c, x], 0.0)
@@ -386,14 +377,26 @@
                 if source is not None:
                     following = following + source(c, x)
                 held[i + 2, c, x] = following
+
+        def inner_planes(c, carry):
+            wait_halo(i, held.at[i + 1], c, slice(2, 4))
+            some(c, [None, None] + [held[i + 1, c, x] for x in range(nx)], inside)
+            return carry
+
+        def outer_planes(c, carry):
+            wait_halo(i, held.at[i + 1], c, slice(0, 2))
+            low, high = x_in[i, 0, c], x_in[i, 1, c]
+            low, high = jnp.where(slab > 0, low, 0.0), jnp.where(slab < slabs - 1, high, 0.0)
+            some(c, [low[0], low[1]] + [held[i + 1, c, x] for x in range(nx)] + [high[0], high[1]], outside)
             if send is not None:
                 @pl.when(send)
                 def _():
-                    start_y(i + 1, held.at[i + 2], c)
+                    start_halo(i + 1, held.at[i + 2], c)
 
             return carry
 
-        lax.fori_loop(0, 3, one, 0)
+        lax.fori_loop(0, 3, inner_planes, 0)
+        lax.fori_loop(0, 3, outer_planes, 0)
 
     wide = 2 * HALF * HALF
     core = lax.rem(comp, 2)

time: 38.7 us -> 38.6 us (level)
  no operation moved by 1% of the time
where the time goes in v10:
time: 38.6 us; the launch traced here: 38.3 us
  Pallas kernels  36.7 us (95%)
  local copies, waits for them, and re-layouts  0.96 us (2%)
  between operations  0.64 us (2%)
    pallas_call x1, Pallas kernels, local(): pl.pallas_call(functools.partial(wave_kernel, (in_x, in_z, in_y, in_group...  36.7 us
    squeeze x1, local copies, waits for them, and re-layouts, local(): return (held[STEPS + 1], held[STEPS])  0.96 us

profile of v10, /device:TPU:0, one launch (start us, length us, event | category | flops | bytes accessed | tf_op | source)
XLA Modules:
  0.0 38.3 jit_solution(15141024802831204169)
XLA Ops:
  0.6 36.7 %shard_map.149 = f32[5,3,8,16,256]{4,3,2,1,0:T(8,128)S(1)} custom-call(f32[3,8,16,256]{3,2,1,0:T(8,128)} %current_in.1, f32[3,8,16,256]{3,2,1,0:T(8,128)} %earlier_in.1, f32[8,16,256]{2,1,0:T(8,128)} %coef_in.1, s32[8,16,256]{2,1,0:T(8,128)} %mask_in.1, s32[1,1024]{1,0:T(1,128)} %bitcast.9, f32[3,1024]{1,0:T(4,128)} %xyz_in.1, s32[1,1024]{1,0:T(1,128)} %bitcast.10, ...), custom_call_target="tpu_custom_call" | custom-call | tf_op jit(solution)/shard_map/pallas_call | solution.py:520
  37.4 1.0 %slice_bitcast_fusion = (f32[3,8,16,256]{3,2,1,0:T(8,128)}, f32[3,8,16,256]{3,2,1,0:T(8,128)}) fusion(f32[5,3,8,16,256]{4,3,2,1,0:T(8,128)S(1)} %shard_map.149), kind=kLoop, calls=%fused_computation | loop fusion | bytes 1572864 | tf_op jit(solution)/shard_map/squeeze | solution.py:554

commit v11 on v10

--- a/solution.py
+++ b/solution.py
@@ -411,7 +411,7 @@
         mode_sums(comps[i], weight[...], column[...], odd, q, p_hi, p_lo)
         f_ref[core] += mode_products(q, p_hi, p_lo)
 
-        @pl.when(i == 2)
+        @pl.when(i == 1)
         def _():
             wait_hop(0)
             start_hop(1)

time: 38.6 us -> 39 us (1.010); the launches traced: 38.3 us -> 38.3 us
  no operation moved by 1% of the time
where the time goes in v11:
time: 39 us; the launch traced here: 38.3 us
  Pallas kernels  36.7 us (94%)
  local copies, waits for them, and re-layouts  0.96 us (2%)
  between operations  0.64 us (2%)
    pallas_call x1, Pallas kernels, local(): pl.pallas_call(functools.partial(wave_kernel, (in_x, in_z, in_y, in_group...  36.7 us
    squeeze x1, local copies, waits for them, and re-layouts, local(): return (held[STEPS + 1], held[STEPS])  0.96 us

profile of v11, /device:TPU:0, one launch (start us, length us, event | category | flops | bytes accessed | tf_op | source)
XLA Modules:
  0.0 38.3 jit_solution(10533593016577717959)
XLA Ops:
  0.6 36.7 %shard_map.149 = f32[5,3,8,16,256]{4,3,2,1,0:T(8,128)S(1)} custom-call(f32[3,8,16,256]{3,2,1,0:T(8,128)} %current_in.1, f32[3,8,16,256]{3,2,1,0:T(8,128)} %earlier_in.1, f32[8,16,256]{2,1,0:T(8,128)} %coef_in.1, s32[8,16,256]{2,1,0:T(8,128)} %mask_in.1, s32[1,1024]{1,0:T(1,128)} %bitcast.9, f32[3,1024]{1,0:T(4,128)} %xyz_in.1, s32[1,1024]{1,0:T(1,128)} %bitcast.10, ...), custom_call_target="tpu_custom_call" | custom-call | tf_op jit(solution)/shard_map/pallas_call | solution.py:520
  37.3 1.0 %slice_bitcast_fusion = (f32[3,8,16,256]{3,2,1,0:T(8,128)}, f32[3,8,16,256]{3,2,1,0:T(8,128)}) fusion(f32[5,3,8,16,256]{4,3,2,1,0:T(8,128)S(1)} %shard_map.149), kind=kLoop, calls=%fused_computation | loop fusion | bytes 1572864 | tf_op jit(solution)/shard_map/squeeze | solution.py:554

commit v12 on v10

--- a/solution.py
+++ b/solution.py
@@ -344,9 +344,9 @@
             copy.wait()
 
     pl.semaphore_wait(barrier, len(partners))
-    start_hop(0)
     for d in range(1, in_group):
         comp_copy(d).start()
+    start_hop(0)
     for c in range(3):
         start_halo(0, held.at[1], c)
     for load in loads[9:]:

time: 38.6 us -> 38.6 us (level)
  no operation moved by 1% of the time
where the time goes in v12:
time: 38.6 us; the launch traced here: 38.4 us
  Pallas kernels  36.8 us (95%)
  local copies, waits for them, and re-layouts  0.96 us (2%)
  between operations  0.64 us (2%)
    pallas_call x1, Pallas kernels, local(): pl.pallas_call(functools.partial(wave_kernel, (in_x, in_z, in_y, in_group...  36.8 us
    squeeze x1, local copies, waits for them, and re-layouts, local(): return (held[STEPS + 1], held[STEPS])  0.96 us

profile of v12, /device:TPU:0, one launch (start us, length us, event | category | flops | bytes accessed | tf_op | source)
XLA Modules:
  0.0 38.4 jit_solution(13372153874228233999)
XLA Ops:
  0.6 36.8 %shard_map.149 = f32[5,3,8,16,256]{4,3,2,1,0:T(8,128)S(1)} custom-call(f32[3,8,16,256]{3,2,1,0:T(8,128)} %current_in.1, f32[3,8,16,256]{3,2,1,0:T(8,128)} %earlier_in.1, f32[8,16,256]{2,1,0:T(8,128)} %coef_in.1, s32[8,16,256]{2,1,0:T(8,128)} %mask_in.1, s32[1,1024]{1,0:T(1,128)} %bitcast.9, f32[3,1024]{1,0:T(4,128)} %xyz_in.1, s32[1,1024]{1,0:T(1,128)} %bitcast.10, ...), custom_call_target="tpu_custom_call" | custom-call | tf_op jit(solution)/shard_map/pallas_call | solution.py:520
  37.4 1.0 %slice_bitcast_fusion = (f32[3,8,16,256]{3,2,1,0:T(8,128)}, f32[3,8,16,256]{3,2,1,0:T(8,128)}) fusion(f32[5,3,8,16,256]{4,3,2,1,0:T(8,128)S(1)} %shard_map.149), kind=kLoop, calls=%fused_computation | loop fusion | bytes 1572864 | tf_op jit(solution)/shard_map/squeeze | solution.py:554
